TPU v7x, 512 devices: a whole 4x8x8 slice. The times are simulated.
512 devices in a mesh: lat: 16 (over z, core), lon: 32 (over x, y).
Axes of the slice: x: 4, y: 8, z: 8, core: 2. Of those that a mesh axis runs over, the one named last changes fastest.
Arguments:
- activation: bfloat16 [256, 256, 256], P('lat', 'lon'), may hold values from -6 to 6
- basis_table: bfloat16 [9, 256, 5, 17], replicated, may hold values from -1 to 1
- lat_depth: int32 [256], replicated, may hold values from 1 to 2, as said below
- lon_extent: int32 [256], replicated, may hold values from 1 to 8, as said below
- weight_one: bfloat16 [9, 256, 256], P(None, 'lon'), may hold values from -0.125 to 0.125
- weight_two: bfloat16 [9, 256, 256], P(None, 'lon'), may hold values from -0.125 to 0.125
- cotangent: bfloat16 [256, 256, 256], P('lat', 'lon'), may hold values from -6 to 6
Outputs:
- output: bfloat16 [256, 256, 256], P('lat', 'lon')
- grad_field: bfloat16 [256, 256, 256], P('lat', 'lon')
- grad_one: float32 [9, 256, 256], P(None, 'lon')
- grad_two: float32 [9, 256, 256], P(None, 'lon')
Inputs may be any that keep to these rules, and one draw needn't show every extreme that they name: `lat_depth`: the row at index 128 has depth 2. `lon_extent`: the rows nearest the poles reach 8.
All inputs are finite; a program needn't handle non-finite values.
Results may differ from a plain program's by a relative error of at most 0.033.
Values may be sent and summed in bfloat16 or wider, within the bound.
A program may use at most 64 MiB of HBM per device.

v0:
```python
import jax
import jax.numpy as jnp
from jax import lax
from jax.sharding import PartitionSpec as P


def padded_2(block, sides, width, periodic):
    for axis, dim in sides:
        count = lax.axis_size(axis)
        forward = [(i, i + 1) for i in range(count - 1)]
        if periodic:
            forward.append((count - 1, 0))
        backward = [(target, source) for source, target in forward]
        low = lax.ppermute(
            lax.slice_in_dim(block, block.shape[dim] - width, None, axis=dim), axis, forward
        )
        high = lax.ppermute(lax.slice_in_dim(block, 0, width, axis=dim), axis, backward)
        block = jnp.concatenate([low, block, high], axis=dim)
    return block


def masked_basis(basis_table, lat_depth, lon_extent):
    lat_span = basis_table.shape[2]
    lon_span = basis_table.shape[3]
    lat_offset = jnp.abs(jnp.arange(lat_span, dtype=jnp.int32) - (lat_span - 1) // 2)
    lon_offset = jnp.abs(jnp.arange(lon_span, dtype=jnp.int32) - (lon_span - 1) // 2)
    inside = (lat_offset[None, :, None] <= lat_depth[:, None, None]) & (
        lon_offset[None, None, :] <= lon_extent[:, None, None]
    )
    return basis_table * inside.astype(basis_table.dtype)[None]


def toeplitz(coef_rows, lon_cols, forward_sense):
    lon_span = coef_rows.shape[-1]
    lon_radius = (lon_span - 1) // 2
    out_index = jnp.arange(lon_cols, dtype=jnp.int32)[:, None]
    in_index = jnp.arange(lon_cols + lon_span - 1, dtype=jnp.int32)[None, :]
    offsets = jnp.arange(lon_span, dtype=jnp.int32)[:, None, None]
    if forward_sense:
        pattern = (in_index - out_index)[None] == offsets
    else:
        pattern = (out_index + 2 * lon_radius - in_index)[None] == offsets
    return jnp.einsum(
        "kiab,bjm->kiajm", coef_rows.astype(jnp.float32), pattern.astype(jnp.float32)
    ).astype(jnp.bfloat16)


def widen_field(values, lat_radius, lon_radius):
    rows_ext = padded_2(values, (("lat", 0),), lat_radius, False)
    return padded_2(rows_ext, (("lon", 1),), lon_radius, True)


def forward_layer(values, weight, forward_map, lat_radius, lon_radius):
    lat_rows = values.shape[0]
    padded = widen_field(values, lat_radius, lon_radius)
    stacked = jnp.stack(
        [padded[lat_step : lat_step + lat_rows] for lat_step in range(2 * lat_radius + 1)], axis=1
    )
    mixed_in = jnp.einsum(
        "kiajm,iamc->kijc", forward_map, stacked, preferred_element_type=jnp.float32
    ).astype(jnp.bfloat16)
    response = jnp.einsum(
        "kijc,kcd->ijd",
        mixed_in,
        lax.all_gather(weight, "lon", axis=1, tiled=True),
        preferred_element_type=jnp.float32,
    )
    output = (values.astype(jnp.float32) + jax.nn.gelu(response)).astype(jnp.bfloat16)
    return (output, mixed_in, response, None)


def back_mix(slope_grad, weight):
    return jnp.einsum(
        "ijd,kcd->kijc",
        slope_grad,
        lax.all_gather(weight, "lon", axis=1, tiled=True),
        preferred_element_type=jnp.float32,
    ).astype(jnp.bfloat16)


def backward_layer(field_grad, mixed_in, response, weight, adjoint_map, lat_radius, lon_radius):
    lat_rows = field_grad.shape[0]
    slope_grad = jax.vjp(jax.nn.gelu, response)[1](field_grad.astype(jnp.float32))[0].astype(
        jnp.bfloat16
    )
    partial_grad = jnp.einsum(
        "kijc,ijd->kcd", mixed_in, slope_grad, preferred_element_type=jnp.float32
    )
    lon_total = lax.psum_scatter(
        partial_grad.astype(jnp.bfloat16), "lon", scatter_dimension=1, tiled=True
    )
    weight_grad = lax.psum(lon_total, "lat").astype(jnp.float32)
    grad_local = back_mix(slope_grad, weight)
    grad_rows = padded_2(grad_local, (("lat", 1),), lat_radius, False)
    grad_wide = padded_2(grad_rows, (("lon", 2),), lon_radius, True)
    adjoint = jnp.zeros(field_grad.shape, jnp.float32)
    for lat_step in range(2 * lat_radius + 1):
        row_first = 2 * lat_radius - lat_step
        section = grad_wide[:, row_first : row_first + lat_rows]
        adjoint = adjoint + jnp.einsum(
            "kijm,kimc->ijc",
            adjoint_map[:, :, lat_step],
            section,
            preferred_element_type=jnp.float32,
        )
    new_grad = (field_grad.astype(jnp.float32) + adjoint).astype(jnp.bfloat16)
    return (new_grad, weight_grad)


def local(activation, basis_table, lat_depth, lon_extent, weight_one, weight_two, cotangent):
    lat_rows = activation.shape[0]
    lon_cols = activation.shape[1]
    lat_span = basis_table.shape[2]
    lat_radius = (lat_span - 1) // 2
    lon_radius = (basis_table.shape[3] - 1) // 2
    coefficient = masked_basis(basis_table, lat_depth, lon_extent)
    coef_pad = jnp.pad(coefficient, ((0, 0), (lat_radius, lat_radius), (0, 0), (0, 0)))
    first_row = lax.axis_index("lat") * lat_rows
    coef_window = lax.dynamic_slice_in_dim(coef_pad, first_row, lat_rows + 2 * lat_radius, 1)
    forward_map = toeplitz(coef_window[:, lat_radius : lat_radius + lat_rows], lon_cols, True)
    adjoint_rows = jnp.stack(
        [
            coef_window[
                :, 2 * lat_radius - lat_step : 2 * lat_radius - lat_step + lat_rows, lat_step
            ]
            for lat_step in range(lat_span)
        ],
        axis=2,
    )
    adjoint_map = toeplitz(adjoint_rows, lon_cols, False)
    hidden, mixed_one, response_one, whole_one = forward_layer(
        activation, weight_one, forward_map, lat_radius, lon_radius
    )
    output, mixed_two, response_two, whole_two = forward_layer(
        hidden, weight_two, forward_map, lat_radius, lon_radius
    )
    grad_hidden, grad_two = backward_layer(
        cotangent, mixed_two, response_two, weight_two, adjoint_map, lat_radius, lon_radius
    )
    grad_field, grad_one = backward_layer(
        grad_hidden, mixed_one, response_one, weight_one, adjoint_map, lat_radius, lon_radius
    )
    return (output, grad_field, grad_one, grad_two)


def solution(mesh):
    placed = (
        P("lat", "lon", None),
        P(),
        P(),
        P(),
        P(None, "lon", None),
        P(None, "lon", None),
        P("lat", "lon", None),
    )
    return jax.shard_map(
        local,
        mesh=mesh,
        in_specs=placed,
        out_specs=(
            P("lat", "lon", None),
            P("lat", "lon", None),
            P(None, "lon", None),
            P(None, "lon", None),
        ),
        check_vma=False,
    )
```

profile of v0, /device:TPU:1, one launch (start us, length us, event | category | flops | bytes accessed | tf_op | source)
XLA Modules:
  0.0 731.7 jit_solution(2968603065424874146)
XLA Ops:
  7.2 0.7 all-gather.3.cloned.1.call-update
  8.0 0.7 fusion.179
  8.7 8.8 %collective-permute-start.1 = (bf16[2,8,256]{2,1,0:T(8,128)(2,1)S(1)}, bf16[2,8,256]{2,1,0:T(8,128)(2,1)S(1)}, u32[]{:S(2)}, u32[]{:S(2)}) collective-permute-start(bf16[2,8,256]{2,1,0:T(8,128)(2,1)S(1)} %get-tuple-element.17), channel_id=1, source_target_pairs={{32,0},{64,32},{96,64},{128,96},{160,128},{192,160},{224,192},{256... | collective-permute-start | bytes 24584 | tf_op jit(solution)/shard_map/ppermute | solution.py:17
  17.5 1.9 collective-permute-start
  19.6 3.8 copy.39
  23.8 2.2 broadcast_multiply_fusion
  26.0 1.7 convolution_convert_fusion.1
  27.7 0.8 copy-done.4
  28.5 4.0 collective-permute-start.3
  32.6 1.9 collective-permute-start.2
  34.6 6.7 collective-permute-done.2
  41.5 2.9 fusion.28
  44.4 44.9 %all-gather.3.cloned.1.call-done = bf16[9,256,256]{2,1,0:T(8,128)(2,1)} async-done(((bf16[9,8,256]{2,1,0:T(8,128)(2,1)}), bf16[9,256,256]{2,1,0:T(8,128)(2,1)}) %all-gather.3.cloned.1.call-update) | async-done | bytes 1179664 | tf_op jit(solution)/shard_map/all_gather | solution.py:65
  89.3 2.8 add_convert_fusion.1
  92.1 7.8 %collective-permute-start.4 = (bf16[2,8,256]{2,1,0:T(8,128)(2,1)S(1)}, bf16[2,8,256]{2,1,0:T(8,128)(2,1)S(1)}, u32[]{:S(2)}, u32[]{:S(2)}) collective-permute-start(bf16[2,8,256]{2,1,0:T(8,128)(2,1)S(1)} %get-tuple-element.15), channel_id=1, source_target_pairs={{0,32},{32,64},{64,96},{96,128},{128,160},{160,192},{192,224},{224... | collective-permute-start | bytes 24584 | tf_op jit(solution)/shard_map/ppermute | solution.py:14
  99.9 1.9 collective-permute-start.5
  101.9 3.0 collective-permute-done.5
  104.9 6.5 collective-permute-start.7
  111.4 1.9 collective-permute-start.6
  113.4 6.6 collective-permute-done.6
  120.2 2.9 fusion.31
  123.1 45.4 %all-gather.5.cloned.1.call-done = bf16[9,256,256]{2,1,0:T(8,128)(2,1)} async-done(((bf16[9,8,256]{2,1,0:T(8,128)(2,1)}), bf16[9,256,256]{2,1,0:T(8,128)(2,1)}) %all-gather.5.cloned.1.call-update) | async-done | bytes 1179664 | tf_op jit(solution)/shard_map/all_gather | solution.py:65
  168.5 2.8 add_convert_fusion
  171.3 1.4 fusion.34
  172.7 7.8 %collective-permute-start.8 = (bf16[9,2,8,256]{3,2,0,1:T(8,128)(2,1)S(1)}, bf16[9,2,8,256]{3,2,0,1:T(8,128)(2,1)S(1)}, u32[]{:S(2)}, u32[]{:S(2)}) collective-permute-start(bf16[9,2,8,256]{3,2,0,1:T(8,128)(2,1)S(1)} %get-tuple-element.13), channel_id=1, source_target_pairs={{0,32},{32,64},{64,96},{96,128},{128,160},{160,192},{192,224},{224... | collective-permute-start | bytes 221192 | tf_op jit(solution)/shard_map/ppermute | solution.py:14
  180.6 2.1 collective-permute-start.9
  183.3 3.1 collective-permute-done.9
  186.5 6.4 collective-permute-start.11
  192.9 1.9 collective-permute-start.10
  195.5 1.2 copy.98
  197.8 9.4 %collective-permute-done.11 = bf16[9,20,8,256]{3,2,0,1:T(8,128)(2,1)S(1)} collective-permute-done((bf16[9,20,8,256]{3,2,0,1:T(8,128)(2,1)S(1)}, bf16[9,20,8,256]{3,2,0,1:T(8,128)(2,1)S(1)}, u32[]{:S(2)}, u32[]{:S(2)}) %collective-permute-start.11) | collective-permute-done | bytes 737312 | tf_op jit(solution)/shard_map/ppermute | solution.py:17
  207.1 7.5 %collective-permute-done.10 = bf16[9,20,8,256]{3,2,0,1:T(8,128)(2,1)S(1)} collective-permute-done((bf16[9,20,8,256]{3,2,0,1:T(8,128)(2,1)S(1)}, bf16[9,20,8,256]{3,2,0,1:T(8,128)(2,1)S(1)}, u32[]{:S(2)}, u32[]{:S(2)}) %collective-permute-start.10) | collective-permute-done | bytes 737312 | tf_op jit(solution)/shard_map/ppermute | solution.py:14
  218.3 1.1 copy.97
  220.6 4.6 collective-permute-start.12
  225.1 1.9 collective-permute-start.13
  227.1 3.7 collective-permute-done.13
  230.9 2.1 collective-permute-start.15
  233.0 3.4 collective-permute-start.14
  236.3 14.3 %collective-permute-done.15 = bf16[9,20,8,256]{3,2,0,1:T(8,128)(2,1)S(1)} collective-permute-done((bf16[9,20,8,256]{3,2,0,1:T(8,128)(2,1)S(1)}, bf16[9,20,8,256]{3,2,0,1:T(8,128)(2,1)S(1)}, u32[]{:S(2)}, u32[]{:S(2)}) %collective-permute-start.15) | collective-permute-done | bytes 737312 | tf_op jit(solution)/shard_map/ppermute | solution.py:17
  250.6 4.9 collective-permute-done.14
  258.2 140.2 %reduce-scatter.9.cloned.1.call-done = bf16[8,2304]{1,0:T(8,128)(2,1)} async-done(((bf16[256,2304]{1,0:T(8,128)(2,1)}), bf16[8,2304]{1,0:T(8,128)(2,1)}) %reduce-scatter.9.cloned.1.call-update) | async-done | bytes 36880
  398.5 0.8 reshape.149
  399.9 209.2 %reduce-scatter.7.cloned.1.call-done = bf16[8,2304]{1,0:T(8,128)(2,1)} async-done(((bf16[256,2304]{1,0:T(8,128)(2,1)}), bf16[8,2304]{1,0:T(8,128)(2,1)}) %reduce-scatter.7.cloned.1.call-update) | async-done | bytes 36880
  609.1 0.8 reshape.147
  610.6 1.1 fusion.114
  611.7 110.7 %all-reduce.4.cloned.1.call-done = (bf16[9,8,256]{2,1,0:T(8,128)(2,1)}, bf16[9,8,256]{2,1,0:T(8,128)(2,1)}) async-done(((bf16[9,8,256]{2,1,0:T(8,128)(2,1)}, bf16[9,8,256]{2,1,0:T(8,128)(2,1)}), (bf16[9,8,256]{2,1,0:T(8,128)(2,1)}, bf16[9,8,256]{2,1,0:T(8,128)(2,1)})) %all-reduce.4.cloned.1.call-update) | async-done | bytes 73744 | tf_op jit(solution)/shard_map/psum | solution.py:92
  722.4 1.4 convert_element_type.109
  723.8 1.4 convert_element_type.111
  (115 shorter events, 12.3 us)
Async XLA Ops:
  7.2 16.2 %copy-start.22 = (s32[256]{0:T(256)S(1)}, s32[256]{0:T(256)}, u32[]{:S(2)}) copy-start(s32[256]{0:T(256)} %param.9) | copy-start | bytes 3076
  7.2 16.3 %copy-start.23 = (s32[256]{0:T(256)S(1)}, s32[256]{0:T(256)}, u32[]{:S(2)}) copy-start(s32[256]{0:T(256)} %param.10) | copy-start | bytes 3076
  7.2 82.1 %all-gather.3.cloned.1.call-start = ((), (), s32[]{:S(2)}) async-start(), calls=%async_computation.2 | async-start | bytes 1216512 | tf_op jit(solution)/shard_map/all_gather | solution.py:65
  7.9 160.6 %all-gather.5.cloned.1.call-start = ((), (), s32[]{:S(2)}) async-start(), calls=%async_computation.3 | async-start | bytes 1216512 | tf_op jit(solution)/shard_map/all_gather | solution.py:65
  8.7 19.8 %collective-permute-start.1 = (bf16[2,8,256]{2,1,0:T(8,128)(2,1)S(1)}, bf16[2,8,256]{2,1,0:T(8,128)(2,1)S(1)}, u32[]{:S(2)}, u32[]{:S(2)}) collective-permute-start(bf16[2,8,256]{2,1,0:T(8,128)(2,1)S(1)} %get-tuple-element.17), channel_id=1, source_target_pairs={{32,0},{64,32},{96,64},{128,96},{160,128},{192,160},{224,192},{256... | collective-permute-start | bytes 24584 | tf_op jit(solution)/shard_map/ppermute | solution.py:17
  17.5 10.2 %collective-permute-start = (bf16[2,8,256]{2,1,0:T(8,128)(2,1)S(1)}, bf16[2,8,256]{2,1,0:T(8,128)(2,1)S(1)}, u32[]{:S(2)}, u32[]{:S(2)}) collective-permute-start(bf16[2,8,256]{2,1,0:T(8,128)(2,1)S(1)} %get-tuple-element.18), channel_id=1, source_target_pairs={{0,32},{32,64},{64,96},{96,128},{128,160},{160,192},{192,224},{224... | collective-permute-start | bytes 24584 | tf_op jit(solution)/shard_map/ppermute | solution.py:14
  19.4 379.0 %reduce-scatter.9.cloned.1.call-start = ((), (), s32[]{:S(2)}) async-start(), calls=%async_computation.5 | async-start | bytes 1216512
  27.7 0.8 copy-start.4
  28.5 12.9 %copy-start.2 = (bf16[9,16,5,8,24]{4,1,3,2,0:T(8,128)(2,1)S(1)}, bf16[9,16,5,8,24]{4,1,3,2,0:T(8,128)(2,1)}, u32[]{:S(2)}) copy-start(bf16[9,16,5,8,24]{4,1,3,2,0:T(8,128)(2,1)} %convolution_convert_fusion.1) | copy-start | bytes 829444
  28.5 6.0 collective-permute-start.3
  32.6 8.7 %collective-permute-start.2 = (bf16[20,8,256]{2,1,0:T(8,128)(2,1)S(1)}, bf16[20,8,256]{2,1,0:T(8,128)(2,1)S(1)}, u32[]{:S(2)}, u32[]{:S(2)}) collective-permute-start(bf16[20,8,256]{2,1,0:T(8,128)(2,1)S(1)} %constant_dynamic-update-slice_fusion), channel_id=1, source_target_pairs={{0,1},{1,2},{2,3},{3,4},{4,5},{5,6},{6,7},{7,8},{8,9},{9,10},{10,1... | collective-permute-start | bytes 245768 | tf_op jit(solution)/shard_map/ppermute | solution.py:14
  92.1 9.8 %collective-permute-start.4 = (bf16[2,8,256]{2,1,0:T(8,128)(2,1)S(1)}, bf16[2,8,256]{2,1,0:T(8,128)(2,1)S(1)}, u32[]{:S(2)}, u32[]{:S(2)}) collective-permute-start(bf16[2,8,256]{2,1,0:T(8,128)(2,1)S(1)} %get-tuple-element.15), channel_id=1, source_target_pairs={{0,32},{32,64},{64,96},{96,128},{128,160},{160,192},{192,224},{224... | collective-permute-start | bytes 24584 | tf_op jit(solution)/shard_map/ppermute | solution.py:14
  99.9 5.0 collective-permute-start.5
  104.9 15.3 %copy-start.3 = (bf16[9,16,5,8,24]{4,1,3,2,0:T(8,128)(2,1)S(1)}, bf16[9,16,5,8,24]{4,1,3,2,0:T(8,128)(2,1)}, u32[]{:S(2)}) copy-start(bf16[9,16,5,8,24]{4,1,3,2,0:T(8,128)(2,1)} %convolution_convert_fusion.1) | copy-start | bytes 829444
  104.9 8.5 %collective-permute-start.7 = (bf16[20,8,256]{2,1,0:T(8,128)(2,1)S(1)}, bf16[20,8,256]{2,1,0:T(8,128)(2,1)S(1)}, u32[]{:S(2)}, u32[]{:S(2)}) collective-permute-start(bf16[20,8,256]{2,1,0:T(8,128)(2,1)S(1)} %pad_maximum_fusion.6), channel_id=1, source_target_pairs={{1,0},{2,1},{3,2},{4,3},{5,4},{6,5},{7,6},{8,7},{9,8},{10,9},{11,1... | collective-permute-start | bytes 245768 | tf_op jit(solution)/shard_map/ppermute | solution.py:17
  111.4 8.6 %collective-permute-start.6 = (bf16[20,8,256]{2,1,0:T(8,128)(2,1)S(1)}, bf16[20,8,256]{2,1,0:T(8,128)(2,1)S(1)}, u32[]{:S(2)}, u32[]{:S(2)}) collective-permute-start(bf16[20,8,256]{2,1,0:T(8,128)(2,1)S(1)} %pad_maximum_fusion.6), channel_id=1, source_target_pairs={{0,1},{1,2},{2,3},{3,4},{4,5},{5,6},{6,7},{7,8},{8,9},{9,10},{10,1... | collective-permute-start | bytes 245768 | tf_op jit(solution)/shard_map/ppermute | solution.py:14
  113.4 9.7 %copy-start.17 = (bf16[9,16,5,17]{3,1,2,0:T(8,128)(2,1)}, bf16[9,16,5,17]{3,1,2,0:T(8,128)(2,1)S(1)}, u32[]{:S(2)}) copy-start(bf16[9,16,5,17]{3,1,2,0:T(8,128)(2,1)S(1)} %constant_dynamic-update-slice_fusion.4) | copy-start | bytes 73444
  168.5 2.9 copy-start.1
  172.7 10.6 %collective-permute-start.8 = (bf16[9,2,8,256]{3,2,0,1:T(8,128)(2,1)S(1)}, bf16[9,2,8,256]{3,2,0,1:T(8,128)(2,1)S(1)}, u32[]{:S(2)}, u32[]{:S(2)}) collective-permute-start(bf16[9,2,8,256]{3,2,0,1:T(8,128)(2,1)S(1)} %get-tuple-element.13), channel_id=1, source_target_pairs={{0,32},{32,64},{64,96},{96,128},{128,160},{160,192},{192,224},{224... | collective-permute-start | bytes 221192 | tf_op jit(solution)/shard_map/ppermute | solution.py:14
  180.6 14.3 %copy-start.6 = (bf16[9,16,8,256]{3,0,2,1:T(8,128)(2,1)S(1)}, bf16[9,16,8,256]{3,0,2,1:T(8,128)(2,1)}, u32[]{:S(2)}) copy-start(bf16[9,16,8,256]{3,0,2,1:T(8,128)(2,1)} %fusion.31) | copy-start | bytes 1769476
  180.6 14.3 %copy-start.20 = (bf16[16,8,256]{2,1,0:T(8,128)(2,1)S(1)}, bf16[16,8,256]{2,1,0:T(8,128)(2,1)}, u32[]{:S(2)}) copy-start(bf16[16,8,256]{2,1,0:T(8,128)(2,1)} %param.13) | copy-start | bytes 196612
  180.6 5.8 collective-permute-start.9
  183.3 11.5 %copy-start.13 = (bf16[9,2,8,256]{3,2,0,1:T(8,128)(2,1)}, bf16[9,2,8,256]{3,2,0,1:T(8,128)(2,1)S(1)}, u32[]{:S(2)}) copy-start(bf16[9,2,8,256]{3,2,0,1:T(8,128)(2,1)S(1)} %collective-permute-done.8) | copy-start | bytes 221188
  186.4 8.4 %copy-start.15 = (bf16[9,2,8,256]{3,2,0,1:T(8,128)(2,1)}, bf16[9,2,8,256]{3,2,0,1:T(8,128)(2,1)S(1)}, u32[]{:S(2)}) copy-start(bf16[9,2,8,256]{3,2,0,1:T(8,128)(2,1)S(1)} %collective-permute-done.9) | copy-start | bytes 221188
  186.5 20.6 %collective-permute-start.11 = (bf16[9,20,8,256]{3,2,0,1:T(8,128)(2,1)S(1)}, bf16[9,20,8,256]{3,2,0,1:T(8,128)(2,1)S(1)}, u32[]{:S(2)}, u32[]{:S(2)}) collective-permute-start(bf16[9,20,8,256]{3,2,0,1:T(8,128)(2,1)S(1)} %pad_maximum_fusion.2), channel_id=1, source_target_pairs={{1,0},{2,1},{3,2},{4,3},{5,4},{6,5},{7,6},{8,7},{9,8},{10,9},{11,1... | collective-permute-start | bytes 2211848 | tf_op jit(solution)/shard_map/ppermute | solution.py:17
  192.9 21.8 %collective-permute-start.10 = (bf16[9,20,8,256]{3,2,0,1:T(8,128)(2,1)S(1)}, bf16[9,20,8,256]{3,2,0,1:T(8,128)(2,1)S(1)}, u32[]{:S(2)}, u32[]{:S(2)}) collective-permute-start(bf16[9,20,8,256]{3,2,0,1:T(8,128)(2,1)S(1)} %pad_maximum_fusion.2), channel_id=1, source_target_pairs={{0,1},{1,2},{2,3},{3,4},{4,5},{5,6},{6,7},{7,8},{8,9},{9,10},{10,1... | collective-permute-start | bytes 2211848 | tf_op jit(solution)/shard_map/ppermute | solution.py:14
  195.5 1.4 copy-start.18
  196.6 18.0 %copy-start.14 = (bf16[9,2,8,256]{3,2,0,1:T(8,128)(2,1)S(1)}, bf16[9,2,8,256]{3,2,0,1:T(8,128)(2,1)}, u32[]{:S(2)}) copy-start(bf16[9,2,8,256]{3,2,0,1:T(8,128)(2,1)} %copy-done.13) | copy-start | bytes 221188
  196.7 18.0 %copy-start.16 = (bf16[9,2,8,256]{3,2,0,1:T(8,128)(2,1)S(1)}, bf16[9,2,8,256]{3,2,0,1:T(8,128)(2,1)}, u32[]{:S(2)}) copy-start(bf16[9,2,8,256]{3,2,0,1:T(8,128)(2,1)} %copy-done.15) | copy-start | bytes 221188
  196.7 412.4 %reduce-scatter.7.cloned.1.call-start = ((), (), s32[]{:S(2)}) async-start(), calls=%async_computation.4 | async-start | bytes 1216512
  197.7 17.4 %copy-start.11 = (bf16[9,16,8,24]{3,1,2,0:T(8,128)(2,1)}, bf16[9,16,8,24]{3,1,2,0:T(8,128)(2,1)S(1)}, u32[]{:S(2)}) copy-start(bf16[9,16,8,24]{3,1,2,0:T(8,128)(2,1)S(1)} %get-tuple-element.7) | copy-start | bytes 165892
  197.7 17.8 %copy-start.9 = (bf16[9,16,8,24]{3,1,2,0:T(8,128)(2,1)}, bf16[9,16,8,24]{3,1,2,0:T(8,128)(2,1)S(1)}, u32[]{:S(2)}) copy-start(bf16[9,16,8,24]{3,1,2,0:T(8,128)(2,1)S(1)} %get-tuple-element.8) | copy-start | bytes 165892
  197.7 18.3 %copy-start.7 = (bf16[9,16,8,24]{3,1,2,0:T(8,128)(2,1)}, bf16[9,16,8,24]{3,1,2,0:T(8,128)(2,1)S(1)}, u32[]{:S(2)}) copy-start(bf16[9,16,8,24]{3,1,2,0:T(8,128)(2,1)S(1)} %get-tuple-element.9) | copy-start | bytes 165892
  216.0 1.0 copy-start.19
  216.0 1.0 copy-start.21
  216.5 1.3 copy-start.5
  218.3 1.7 copy-start
  219.5 502.9 %all-reduce.4.cloned.1.call-start = ((), (), s32[]{:S(2)}) async-start(), calls=%async_computation.6 | async-start | bytes 147456 | tf_op jit(solution)/shard_map/psum | solution.py:92
  220.6 6.5 collective-permute-start.12
  225.1 5.7 collective-permute-start.13
  230.9 25.0 %copy-start.12 = (bf16[9,16,8,24]{3,1,2,0:T(8,128)(2,1)S(1)}, bf16[9,16,8,24]{3,1,2,0:T(8,128)(2,1)}, u32[]{:S(2)}) copy-start(bf16[9,16,8,24]{3,1,2,0:T(8,128)(2,1)} %copy-done.11) | copy-start | bytes 165892
  230.9 19.7 %collective-permute-start.15 = (bf16[9,20,8,256]{3,2,0,1:T(8,128)(2,1)S(1)}, bf16[9,20,8,256]{3,2,0,1:T(8,128)(2,1)S(1)}, u32[]{:S(2)}, u32[]{:S(2)}) collective-permute-start(bf16[9,20,8,256]{3,2,0,1:T(8,128)(2,1)S(1)} %pad_maximum_fusion.3), channel_id=1, source_target_pairs={{1,0},{2,1},{3,2},{4,3},{5,4},{6,5},{7,6},{8,7},{9,8},{10,9},{11,1... | collective-permute-start | bytes 2211848 | tf_op jit(solution)/shard_map/ppermute | solution.py:17
  233.0 22.5 %collective-permute-start.14 = (bf16[9,20,8,256]{3,2,0,1:T(8,128)(2,1)S(1)}, bf16[9,20,8,256]{3,2,0,1:T(8,128)(2,1)S(1)}, u32[]{:S(2)}, u32[]{:S(2)}) collective-permute-start(bf16[9,20,8,256]{3,2,0,1:T(8,128)(2,1)S(1)} %pad_maximum_fusion.3), channel_id=1, source_target_pairs={{0,1},{1,2},{2,3},{3,4},{4,5},{5,6},{6,7},{7,8},{8,9},{9,10},{10,1... | collective-permute-start | bytes 2211848 | tf_op jit(solution)/shard_map/ppermute | solution.py:14
  255.9 1.0 copy-start.10
  255.9 1.4 copy-start.8
Sparse Core Ops, SparseCore 0:
  11.1 78.1 all-gather.2
  92.4 76.0 all-gather.4
  196.8 201.6 reduce-scatter.8
  402.7 206.3 reduce-scatter.6
  611.9 110.4 all-reduce.3
where the time goes:
time: 733 us; the launch traced here: 732 us
  waiting for transfers between devices  610 us (83%)
  starting transfers between devices  65.3 us (9%)
  matrix products  22 us (3%)
  between operations  14.4 us (2%)
  local copies, waits for them, and re-layouts  13.1 us (2%)
    unnamed x7, waiting for transfers between devices  350 us
    psum x1, waiting for transfers between devices, backward_layer(): weight_grad = lax.psum(lon_total, 'lat').astype(jnp.float32)  111 us
    all_gather x2, waiting for transfers between devices, forward_layer(): lax.all_gather(weight, 'lon', axis=1, tiled=True)  90.3 us
    ppermute x8, starting transfers between devices, padded_2(): lax.ppermute(lax.slice_in_dim(block, 0, width, axis=dim), axis, backward)  33.7 us
    ppermute x8, waiting for transfers between devices, padded_2(): lax.ppermute(lax.slice_in_dim(block, 0, width, axis=dim), axis, backward)  33.4 us
    ppermute x8, starting transfers between devices, padded_2(): lax.ppermute(lax.slice_in_dim(block, block.shape[dim] - width, None, axis...  31.2 us
    ppermute x8, waiting for transfers between devices, padded_2(): lax.ppermute(lax.slice_in_dim(block, block.shape[dim] - width, None, axis...  25.7 us
  transfers between devices with their start and end apart: 21, of which 14 were waited for; matrix products, arithmetic and copies ran while one was open for 4% of the time, Pallas kernels for 0%

commit v1 on v0

v1 whole, which is shorter than its diff:
```python
import functools

import jax
import jax.numpy as jnp
from jax import lax
from jax.experimental import pallas as pl
from jax.experimental.pallas import tpu as pltpu
from jax.sharding import PartitionSpec as P

NX, NY, NZ = 4, 8, 8
BASIS = 9
CH = 256
ROWS, COLS = 16, 8
CELLS = ROWS * COLS
GRID = 256
SIDE = (ROWS + 4) * COLS
EXT = 512
OWN = SIDE + 2 * COLS
F32 = jnp.float32
BF16 = jnp.bfloat16
SLOTS = 200


def gelu_and_slope(y):
    c = 0.7978845608028654
    t = jnp.tanh(c * (y + 0.044715 * (y * y * y)))
    cdf = 0.5 * (1.0 + t)
    slope = cdf + 0.5 * y * (1.0 - t * t) * (c * (1.0 + 3.0 * 0.044715 * (y * y)))
    return y * cdf, slope


def kernel(
    act_ref,
    basis_ref,
    depth_ref,
    extent_ref,
    w1_ref,
    w2_ref,
    cot_ref,
    out_ref,
    gfield_ref,
    g1_ref,
    g2_ref,
    bw,
    pad,
    cb,
    t1,
    tmap,
    xs,
    wl,
    wf,
    zb,
    zt,
    zg,
    sg,
    pb,
    ry,
    qy,
    rz,
    fin,
    yb,
    send_sem,
    recv_sem,
    local_sem,
):
    lat = lax.axis_index("lat")
    lon = lax.axis_index("lon")
    z, core = lat // 2, lat % 2
    x, y = lon // NY, lon % NY
    other = 1 - core
    sib = lat + 1 - 2 * core

    def at_x(d):
        return lax.rem(x + d, NX) * NY + y

    def at_y(d):
        return x * NY + lax.rem(y + d + NY, NY)

    def at_z(d):
        return lax.rem(z + d, NZ) * 2 + core

    n_lat, n_lon = 2 * NZ, NX * NY
    lat_up, lat_dn = lax.rem(lat + n_lat - 1, n_lat), lax.rem(lat + 1, n_lat)
    lon_lf, lon_rt = lax.rem(lon + n_lon - 1, n_lon), lax.rem(lon + 1, n_lon)

    barrier = pltpu.get_barrier_semaphore()
    peers = [(sib, lon)]
    peers += [(lat, at_x(d)) for d in range(1, NX)] + [(sib, at_x(d)) for d in range(1, NX)]
    peers += [(lat, at_y(d)) for d in range(1, NY)] + [(at_z(d), lon) for d in range(1, NZ)]
    peers += [(a, b) for a in (lat_up, lat, lat_dn) for b in (lon_lf, lon, lon_rt)
              if not (a is lat and b is lon)]
    for peer in peers:
        pl.semaphore_signal(barrier, inc=1, device_id=peer, device_id_type=pl.DeviceIdType.MESH)

    row0 = lat * ROWS
    loads = [
        pltpu.make_async_copy(basis_ref.at[:, pl.ds(row0, ROWS)], bw.at[:, 2:18], local_sem.at[0]),
        pltpu.make_async_copy(
            basis_ref.at[:, pl.ds(lax.rem(row0 + GRID - 2, GRID), 2)], bw.at[:, 0:2], local_sem.at[1]
        ),
        pltpu.make_async_copy(
            basis_ref.at[:, pl.ds(lax.rem(row0 + ROWS, GRID), 2)], bw.at[:, 18:20], local_sem.at[2]
        ),
    ]
    for load in loads:
        load.start()

    sent = []

    def send(src, dst, device):
        slot = len(sent)
        copy = pltpu.make_async_remote_copy(
            src_ref=src,
            dst_ref=dst,
            send_sem=send_sem.at[slot],
            recv_sem=recv_sem.at[slot],
            device_id=device,
            device_id_type=pl.DeviceIdType.MESH,
        )
        copy.start()
        sent.append(copy)
        return copy

    def arrive(copies):
        for copy in copies:
            copy.wait_recv()

    def flat(ref):
        return ref[...].astype(F32).reshape(CELLS, CH)

    xs[:, 3 * SIDE : EXT, :] = jnp.zeros((4, EXT - 3 * SIDE, CH), BF16)
    xs[0, OWN : OWN + CELLS, :] = flat(act_ref).astype(BF16)
    for w, ref in enumerate((w1_ref, w2_ref)):
        wl[w, core, x, y] = ref[:, :, pl.ds(pl.multiple_of(core * 128, 128), 128)]

    pl.semaphore_wait(barrier, len(peers))

    def halo(n):
        own = xs.at[n, OWN : OWN + CELLS]
        top = xs.at[n, OWN : OWN + 16]
        bottom = xs.at[n, OWN + CELLS - 16 : OWN + CELLS]
        lf, mid, rt = 0, SIDE, 2 * SIDE
        low, high = 16, SIDE - 16

        def to(src, base, off, rows, device):
            return send(src, xs.at[n, base + off : base + off + rows], device)

        return [
            to(own, lf, low, CELLS, (lat, lon_rt)),
            to(own, rt, low, CELLS, (lat, lon_lf)),
            to(bottom, mid, 0, 16, (lat_dn, lon)),
            to(top, mid, high, 16, (lat_up, lon)),
            to(bottom, lf, 0, 16, (lat_dn, lon_rt)),
            to(bottom, rt, 0, 16, (lat_dn, lon_lf)),
            to(top, lf, high, 16, (lat_up, lon_rt)),
            to(top, rt, high, 16, (lat_up, lon_lf)),
        ]

    def share(ref):
        return send(ref, ref, (sib, lon))

    def gather_xy(w, k0, nk):
        ks = slice(k0, k0 + nk)

        def col(dy, xa=0, xb=NX):
            return wl.at[w, core, xa:xb, lax.rem(y + dy + NY, NY), ks]

        mine = wl.at[w, core, x, y, ks]
        got = [send(mine, mine, (lat, at_x(d))) for d in range(1, NX)]
        yield
        arrive(got)
        shared = [share(col(0))]
        half = NX // 2
        for t in range(NY // 2):
            if t < NY // 2 - 1:
                up, dn = col(-t), col(t)
                got_up, got_dn = col(-t - 1), col(t + 1)
            else:
                up, dn = col(-t, 0, half), col(t, half, NX)
                got_up, got_dn = col(-t - 1, 0, half), col(t + 1, half, NX)
            got = [send(up, up, (lat, at_y(1))), send(dn, dn, (lat, at_y(-1)))]
            yield
            arrive(got)
            shared += [share(got_up), share(got_dn)]
        yield
        arrive(shared)

    def gather_yx(w, k0, nk):
        ks = slice(k0, k0 + nk)

        def one(dy, a=0, b=nk):
            return wl.at[w, core, x, lax.rem(y + dy + NY, NY), k0 + a : k0 + b]

        half = nk // 2
        for t in range(NY // 2):
            if t < NY // 2 - 1:
                up, dn = one(-t), one(t)
            else:
                up, dn = one(-t, 0, half), one(t, half, nk)
            got = [send(up, up, (lat, at_y(1))), send(dn, dn, (lat, at_y(-1)))]
            yield
            arrive(got)

        def row(d):
            return wl.at[w, core, lax.rem(x + d, NX), :, ks]

        got = [send(row(0), row(0), (lat, at_x(d))) for d in range(1, NX)]
        shared = [share(row(0))]
        yield
        for d in range(1, NX):
            arrive([got[d - 1]])
            shared.append(share(row(NX - d)))
        yield
        arrive(shared)

    def step(*parts):
        for part in parts:
            next(part, None)

    def finish(*parts):
        live = list(parts)
        while live:
            live = [part for part in live if next(part, "end") != "end"]

    in_halo = halo(0)
    w1_parts = (gather_xy(0, 0, 5), gather_yx(0, 5, 4))
    step(*w1_parts)

    for load in loads:
        load.wait()
    pad[...] = jnp.zeros(pad.shape, F32)
    sub = lax.broadcasted_iota(jnp.int32, (8, 128), 0)
    lane = lax.broadcasted_iota(jnp.int32, (8, 128), 1)
    slot_a = (lane * 2731) >> 16

    def coef_row(r, carry):
        row = row0 + r - 2
        wrapped = lax.rem(row + GRID, GRID)
        inside = (
            (jnp.abs(sub - 2) <= depth_ref[wrapped])
            & (jnp.abs(lane - 8) <= extent_ref[wrapped])
            & (row >= 0)
            & (row < GRID)
        )
        for k in range(BASIS):
            pad[r, k, 0:5, 0:17] = bw[k, r].astype(F32)
        for k in range(BASIS):
            tile = jnp.where(inside, pad[r, k], 0.0)
            tile = pltpu.roll(tile, 0, 1, stride=12, stride_axis=0)
            tile = pltpu.roll(tile, 0, 1, stride=12, stride_axis=0)
            cb[r, k] = jnp.broadcast_to(jnp.sum(tile, axis=0, keepdims=True), (8, 128))
        return carry

    lax.fori_loop(0, ROWS + 4, coef_row, 0)
    step(*w1_parts)

    wide_l = lax.broadcasted_iota(jnp.int32, (256, EXT), 0)
    wide_t = lax.broadcasted_iota(jnp.int32, (256, EXT), 1)
    l_q = wide_l >> 7
    l_in = wide_l & 127
    l_a = (l_in * 2731) >> 16
    l_m = l_in - 24 * l_a

    def build(n):
        def pair(p, carry):
            for q in range(2):
                i = 2 * p + q
                row = row0 + i
                for k in range(BASIS):
                    if n == 0:
                        reach = row + slot_a - 2
                        tile = jnp.where((reach >= 0) & (reach < GRID), cb[i + 2, k], 0.0)
                        tile = pltpu.roll(tile, 0, 1, stride=1, stride_axis=0)
                    else:
                        tile = cb[i + 4, k]
                        for a in range(1, 5):
                            tile = jnp.where(slot_a == a, cb[i + 4 - a, k], tile)
                        tile = pltpu.roll(tile, 0, 1, stride=1, stride_axis=0)
                    t1[p, k, 8 * q : 8 * q + 8, 128 * q : 128 * q + 128] = tile
                    t1[p, k, 8 * q : 8 * q + 8, 128 * (1 - q) : 128 * (1 - q) + 128] = jnp.zeros(
                        (8, 128), F32
                    )
            return carry

        if n == 1:
            src = lax.broadcasted_iota(jnp.int32, (128, 128), 0)
            dst = lax.broadcasted_iota(jnp.int32, (128, 128), 1)
            src_a = (src * 2731) >> 16
            mirror = jnp.where(
                (dst == 48 * src_a + 16 - src) & (src - 24 * src_a < 17) & (src_a < 5), 1.0, 0.0
            ).astype(BF16)
            for r in range(0, ROWS + 4, 4):
                rows = cb[r : r + 4].reshape(4 * BASIS * 8, 128).astype(BF16)
                cb[r : r + 4] = jnp.dot(rows, mirror, preferred_element_type=F32).reshape(
                    4, BASIS, 8, 128
                )
        lax.fori_loop(0, 8, pair, 0)
        m = l_m
        shift = l_q + (l_a if n == 0 else 4 - l_a)
        place = jnp.where(
            (wide_t == (m >> 3) * SIDE + 8 * shift + (m & 7)) & (l_a < 5), 1.0, 0.0
        ).astype(BF16)
        for p in range(8):
            spread = jnp.dot(
                t1[p].reshape(16 * BASIS, 256).astype(BF16), place, preferred_element_type=F32
            )
            spread = pltpu.roll(spread, 16 * p, 1) if p else spread
            tmap[n, :, 16 * p : 16 * p + 16, :] = spread.reshape(BASIS, 16, EXT).astype(BF16)

    build(0)
    step(*w1_parts)

    def conv(n, field):
        for k in range(0, BASIS, 3):
            part = jnp.dot(
                tmap[n, k : k + 3].reshape(3 * CELLS, EXT), xs[field], preferred_element_type=F32
            )
            zb[k : k + 3] = part.astype(BF16).reshape(3, CELLS, CH)

    def spread_z(layer):
        for k in range(BASIS):
            zt[layer, k] = zb[k].astype(F32).T.astype(BF16)

        def block(d):
            return zt.at[layer, :, pl.ds(lax.rem(x + d, NX) * 64, 64)]

        zg[layer, x, core] = zt[layer, :, pl.ds(pl.multiple_of(x * 64, 64), 64)]
        got = [send(block(d), zg.at[layer, x, core], (lat, at_x(d))) for d in range(1, NX)]
        yield
        arrive(got)
        mine = zg.at[layer, :, core]
        shared = [send(mine, mine, (sib, lon))]
        yield
        arrive(shared)

    def settle(w):
        for k in range(BASIS):
            for h in range(2):
                wf[w, k, :, h * 128 : (h + 1) * 128] = (
                    wl[w, h, :, :, k].astype(F32).reshape(CH, 128).astype(BF16)
                )

    def mix(w):
        total = jnp.zeros((CELLS, CH), F32)
        for k in range(BASIS):
            total += jnp.dot(zb[k], wf[w, k], preferred_element_type=F32)
        return total

    def mix_back(w):
        total = jnp.zeros((CELLS, CH), F32)
        for k in range(BASIS):
            total += lax.dot_general(
                zb[k], wf[w, k], (((1,), (1,)), ((), ())), preferred_element_type=F32
            )
        return total

    def own_block(n):
        return xs[n, OWN : OWN + CELLS, :].astype(F32)

    arrive(in_halo)
    conv(0, 0)
    step(*w1_parts)
    build(1)
    finish(*w1_parts)
    settle(0)
    w2_parts = (gather_xy(1, 0, 5), gather_yx(1, 5, 4))
    step(*w2_parts)
    y1 = mix(0)
    yb[...] = y1
    hidden = (own_block(0) + gelu_and_slope(y1)[0]).astype(BF16)
    xs[1, OWN : OWN + CELLS, :] = hidden
    mid_halo = halo(1)
    step(*w2_parts)
    z1 = spread_z(0)
    step(z1)
    step(*w2_parts)
    arrive(mid_halo)
    conv(0, 1)
    finish(*w2_parts)
    settle(1)
    y2 = mix(1)
    grown, slope = gelu_and_slope(y2)
    out_ref[...] = (own_block(1) + grown).reshape(ROWS, COLS, CH).astype(BF16)

    def spread_s(layer, n, values):
        xs[n, OWN : OWN + CELLS, :] = values
        around = halo(n)
        for h in range(2):
            @pl.when(core == h)
            def _():
                sg[layer, x, h] = values[:, h * 128 : (h + 1) * 128]

        got = []
        for d in range(NX):
            for dc in range(2):
                if d == 0 and dc == 0:
                    continue
                h = core if dc == 0 else other
                src = xs.at[n, OWN : OWN + CELLS, pl.ds(pl.multiple_of(h * 128, 128), 128)]
                got.append(
                    send(src, sg.at[layer, x, core], (lat if dc == 0 else sib, at_x(d)))
                )
        return around, got

    around2, all_s2 = spread_s(1, 2, (flat(cot_ref) * slope).astype(BF16))
    z2 = spread_z(1)
    step(z2)
    step(z1)
    arrive(around2)
    conv(1, 2)
    grad_hidden = (flat(cot_ref) + mix_back(1)).astype(BF16).astype(F32)
    s1 = (grad_hidden * gelu_and_slope(yb[...])[1]).astype(BF16)
    around1, all_s1 = spread_s(0, 3, s1)
    step(z2)

    def weight_partial(layer):
        total = jnp.zeros((BASIS * 64, 128), F32)
        for a in range(NX):
            left = jnp.concatenate([zg[layer, a, h].reshape(BASIS * 64, 128) for h in range(2)], axis=1)
            total += jnp.dot(left, sg[layer, a].reshape(256, 128), preferred_element_type=F32)
        blocks = total.reshape(BASIS, NY, 8, 128)
        for b in range(NY):
            pb[layer, b] = blocks[:, b].astype(BF16)
        ry[layer, y] = pb[layer, y]
        return [
            send(pb.at[layer, lax.rem(y + d, NY)], ry.at[layer, y], (lat, at_y(d)))
            for d in range(1, NY)
        ]

    def weight_rows(layer, got):
        arrive(got)
        total = jnp.sum(ry[layer].astype(F32), axis=0)
        qy[layer] = total.astype(BF16)
        rz[layer, z] = qy[layer]
        return [send(qy.at[layer], rz.at[layer, z], (at_z(d), lon)) for d in range(1, NZ)]

    def weight_bands(layer, got):
        arrive(got)
        fin[layer, core] = jnp.sum(rz[layer].astype(F32), axis=0)
        mine = fin.at[layer, core]
        return [send(mine, mine, (sib, lon))]

    arrive(all_s2)
    finish(z1, z2)
    p2 = weight_partial(1)
    arrive(all_s1)
    p1 = weight_partial(0)
    arrive(around1)
    conv(1, 3)
    q2 = weight_rows(1, p2)
    gfield_ref[...] = (grad_hidden + mix_back(0)).reshape(ROWS, COLS, CH).astype(BF16)
    q1 = weight_rows(0, p1)
    r2 = weight_bands(1, q2)
    r1 = weight_bands(0, q1)
    for layer, ref, got in ((1, g2_ref, r2), (0, g1_ref, r1)):
        arrive(got)
        for h in range(2):
            ref[:, :, h * 128 : (h + 1) * 128] = fin[layer, h]
    for copy in sent:
        copy.wait_send()


def local(activation, basis_table, lat_depth, lon_extent, weight_one, weight_two, cotangent):
    vmem = pl.BlockSpec(memory_space=pltpu.VMEM)
    smem = pl.BlockSpec(memory_space=pltpu.SMEM)
    field = jax.ShapeDtypeStruct((ROWS, COLS, CH), BF16)
    grad = jax.ShapeDtypeStruct((BASIS, 8, CH), F32)
    return pl.pallas_call(
        kernel,
        out_shape=(field, field, grad, grad),
        in_specs=[vmem, pl.BlockSpec(memory_space=pl.ANY), smem, smem, vmem, vmem, vmem],
        out_specs=(vmem, vmem, vmem, vmem),
        scratch_shapes=[
            pltpu.VMEM((BASIS, ROWS + 4, 5, 17), BF16),
            pltpu.VMEM((ROWS + 4, BASIS, 8, 128), F32),
            pltpu.VMEM((ROWS + 4, BASIS, 8, 128), F32),
            pltpu.VMEM((8, BASIS, 16, 256), F32),
            pltpu.VMEM((2, BASIS, CELLS, EXT), BF16),
            pltpu.VMEM((4, EXT, CH), BF16),
            pltpu.VMEM((2, 2, NX, NY, BASIS, 8, 128), BF16),
            pltpu.VMEM((2, BASIS, CH, CH), BF16),
            pltpu.VMEM((BASIS, CELLS, CH), BF16),
            pltpu.VMEM((2, BASIS, CH, CELLS), BF16),
            pltpu.VMEM((2, NX, 2, BASIS, 64, CELLS), BF16),
            pltpu.VMEM((2, NX, 2, CELLS, 128), BF16),
            pltpu.VMEM((2, NY, BASIS, 8, 128), BF16),
            pltpu.VMEM((2, NY, BASIS, 8, 128), BF16),
            pltpu.VMEM((2, BASIS, 8, 128), BF16),
            pltpu.VMEM((2, NZ, BASIS, 8, 128), BF16),
            pltpu.VMEM((2, 2, BASIS, 8, 128), F32),
            pltpu.VMEM((CELLS, CH), F32),
            pltpu.SemaphoreType.DMA((SLOTS,)),
            pltpu.SemaphoreType.DMA((SLOTS,)),
            pltpu.SemaphoreType.DMA((3,)),
        ],
        compiler_params=pltpu.CompilerParams(
            collective_id=0, has_side_effects=True, vmem_limit_bytes=48 * 1024 * 1024
        ),
        cost_estimate=pl.CostEstimate(flops=10**9, bytes_accessed=10**7, transcendentals=10**5),
    )(activation, basis_table, lat_depth, lon_extent, weight_one, weight_two, cotangent)


def solution(mesh):
    field = P("lat", "lon", None)
    weight = P(None, "lon", None)
    return jax.shard_map(
        local,
        mesh=mesh,
        in_specs=(field, P(), P(), P(), weight, weight, field),
        out_specs=(field, field, weight, weight),
        check_vma=False,
    )
```

time: 733 us -> 104 us (0.14)
  waiting for transfers between devices: 610 us -> 0 us
  Pallas kernels: 0 us -> 92.5 us
  starting transfers between devices: 65.3 us -> 0 us
  matrix products: 22 us -> 0 us
  between operations: 14.4 us -> 0.73 us
    unnamed x7 -> x0, waiting for transfers between devices: 350 us -> none
    psum x1 -> x0, waiting for transfers between devices: 111 us -> none  [backward_layer(): weight_grad = lax.psum(lon_total, 'lat').astype(jnp.float32)]
    pallas_call x0 -> x1, Pallas kernels: none -> 92.5 us  [local(): pl.pallas_call(kernel, out_shape=(field, field, grad, grad), in_specs=[vm...]
    all_gather x2 -> x0, waiting for transfers between devices: 90.3 us -> none  [forward_layer(): lax.all_gather(weight, 'lon', axis=1, tiled=True)]
    ppermute x16 -> x0, starting transfers between devices: 64.9 us -> none  [the longest x8 33.7 us: padded_2(): lax.ppermute(lax.slice_in_dim(block, 0, width, axis=dim), axis, backward)]
    ppermute x16 -> x0, waiting for transfers between devices: 59.2 us -> none  [the longest x8 33.4 us: padded_2(): lax.ppermute(lax.slice_in_dim(block, 0, width, axis=dim), axis, backward)]
    dot_general x20 -> x0, matrix products: 22 us -> none  [the longest x2 5.86 us: forward_layer(): jnp.einsum('kiajm,iamc->kijc', forward_map, stacked, preferred_element_ty...]
  transfers between devices with their start and end apart: 21 -> 0, of which waited for: 14 -> 0; matrix products, arithmetic and copies ran while one was open for 4% -> 0% of each run, Pallas kernels for 0% -> 0%
where the time goes in v1:
time: 104 us; the launch traced here: 103 us
  Pallas kernels  92.5 us (89%)
  local copies, waits for them, and re-layouts  9.99 us (10%)
    pallas_call x1, Pallas kernels, local(): pl.pallas_call(kernel, out_shape=(field, field, grad, grad), in_specs=[vm...  92.5 us
    unnamed x19, local copies, waits for them, and re-layouts  9.99 us

profile of v1, /device:TPU:1, one launch (start us, length us, event | category | flops | bytes accessed | tf_op | source)
XLA Modules:
  0.0 103.2 jit_solution(3956690518466582095)
XLA Ops:
  0.6 0.0 copy-start.2
  0.6 0.0 copy-start.4
  0.7 0.0 copy-start.3
  0.7 0.0 copy-start.6
  0.7 0.0 copy-start.5
  0.7 0.0 copy-start.1
  0.7 5.1 %copy.11.basis_ref = bf16[9,256,5,17]{3,2,1,0:T(8,128)(2,1)} copy(bf16[9,256,5,17]{1,3,2,0:T(8,128)(2,1)} %param.8) | data formatting | bytes 783360 | tf_op args[1]
  5.8 0.0 copy-done.2
  5.8 0.0 copy-done.4
  5.8 0.0 copy-done.3
  5.8 0.0 copy-done.6
  5.8 0.0 copy-done.5
  5.8 0.0 copy-done.1
  5.8 0.0 copy-start
  5.9 2.3 %copy-done = bf16[9,256,5,17]{3,2,1,0:T(8,128)(2,1)S(1)} copy-done((bf16[9,256,5,17]{3,2,1,0:T(8,128)(2,1)S(1)}, bf16[9,256,5,17]{3,2,1,0:T(8,128)(2,1)}, u32[]{:S(2)}) %copy-start) | copy-done | bytes 391704
  8.2 92.5 %shard_map.102 = (bf16[16,8,256]{2,1,0:T(8,128)(2,1)S(1)}, bf16[16,8,256]{2,1,0:T(8,128)(2,1)S(1)}, f32[9,8,256]{2,1,0:T(8,128)S(1)}, f32[9,8,256]{2,1,0:T(8,128)S(1)}) custom-call(bf16[16,8,256]{2,1,0:T(8,128)(2,1)S(1)} %copy-done.1, bf16[9,256,5,17]{3,2,1,0:T(8,128)(2,1)S(1)} %copy-done, s32[256]{0:T(256)S(1)} %copy-done.5, s32[256]{0:T(256)S(1)} %copy-done.6, ...), custom_call_target="tpu_custom_call" | custom-call | flops 1000000000 | bytes 10000000 | tf_op jit(solution)/shard_map/pallas_call | solution.py:468
  100.7 0.6 copy.16
  101.3 0.6 copy.17
  101.9 0.6 copy.18
  102.5 0.6 copy.19
Async XLA Ops:
  0.6 5.2 %copy-start.2 = (bf16[16,8,256]{2,1,0:T(8,128)(2,1)S(1)}, bf16[16,8,256]{2,1,0:T(8,128)(2,1)}, u32[]{:S(2)}) copy-start(bf16[16,8,256]{2,1,0:T(8,128)(2,1)} %cot_ref.1) | copy-start | bytes 196612
  0.6 5.2 %copy-start.4 = (bf16[9,8,256]{2,1,0:T(8,128)(2,1)S(1)}, bf16[9,8,256]{2,1,0:T(8,128)(2,1)}, u32[]{:S(2)}) copy-start(bf16[9,8,256]{2,1,0:T(8,128)(2,1)} %w2_ref.1) | copy-start | bytes 110596
  0.7 5.2 %copy-start.3 = (bf16[9,8,256]{2,1,0:T(8,128)(2,1)S(1)}, bf16[9,8,256]{2,1,0:T(8,128)(2,1)}, u32[]{:S(2)}) copy-start(bf16[9,8,256]{2,1,0:T(8,128)(2,1)} %w1_ref.1) | copy-start | bytes 110596
  0.7 5.2 %copy-start.6 = (s32[256]{0:T(256)S(1)}, s32[256]{0:T(256)}, u32[]{:S(2)}) copy-start(s32[256]{0:T(256)} %extent_ref.1) | copy-start | bytes 3076
  0.7 5.2 %copy-start.5 = (s32[256]{0:T(256)S(1)}, s32[256]{0:T(256)}, u32[]{:S(2)}) copy-start(s32[256]{0:T(256)} %depth_ref.1) | copy-start | bytes 3076
  0.7 5.2 %copy-start.1 = (bf16[16,8,256]{2,1,0:T(8,128)(2,1)S(1)}, bf16[16,8,256]{2,1,0:T(8,128)(2,1)}, u32[]{:S(2)}) copy-start(bf16[16,8,256]{2,1,0:T(8,128)(2,1)} %act_ref.1) | copy-start | bytes 196612
  5.8 2.3 %copy-start = (bf16[9,256,5,17]{3,2,1,0:T(8,128)(2,1)S(1)}, bf16[9,256,5,17]{3,2,1,0:T(8,128)(2,1)}, u32[]{:S(2)}) copy-start(bf16[9,256,5,17]{3,2,1,0:T(8,128)(2,1)} %copy.11.basis_ref) | copy-start | bytes 1175044

commit v2 on v1

v2 whole, which is shorter than its diff:
```python
import jax
import jax.numpy as jnp
from jax import lax
from jax.experimental import pallas as pl
from jax.experimental.pallas import tpu as pltpu
from jax.sharding import PartitionSpec as P

NX, NY, NZ = 4, 8, 8
BASIS = 9
CH = 256
ROWS, COLS = 16, 8
CELLS = ROWS * COLS
GRID = 256
SIDE = (ROWS + 4) * COLS
EXT = 512
OWN = SIDE + 2 * COLS
F32 = jnp.float32
BF16 = jnp.bfloat16
SLOTS = 48
SPLIT = 2
PARTS, DEEP = 3, 3


def gelu_and_slope(y):
    c = 0.7978845608028654
    t = jnp.tanh(c * (y + 0.044715 * (y * y * y)))
    cdf = 0.5 * (1.0 + t)
    slope = cdf + 0.5 * y * (1.0 - t * t) * (c * (1.0 + 3.0 * 0.044715 * (y * y)))
    return y * cdf, slope


def kernel(
    act_ref,
    basis_ref,
    depth_ref,
    extent_ref,
    w1_ref,
    w2_ref,
    cot_ref,
    out_ref,
    gfield_ref,
    g1_ref,
    g2_ref,
    basis,
    depth,
    extent,
    cot,
    pad,
    cb,
    t1,
    tmap,
    xs,
    wl,
    wf,
    zb,
    zt,
    zg,
    sg,
    pb,
    ry,
    qy,
    rz,
    fin,
    yb,
    send_sem,
    recv_sem,
    load_sem,
):
    lat = lax.axis_index("lat")
    lon = lax.axis_index("lon")
    z, core = lat // 2, lat % 2
    x, y = lon // NY, lon % NY
    other = 1 - core
    sib = lat + 1 - 2 * core

    def at_x(d):
        return lax.rem(x + d, NX) * NY + y

    def at_y(d):
        return x * NY + lax.rem(y + d, NY)

    def at_z(d):
        return lax.rem(z + d, NZ) * 2 + core

    n_lat, n_lon = 2 * NZ, NX * NY
    lat_up, lat_dn = lax.rem(lat + n_lat - 1, n_lat), lax.rem(lat + 1, n_lat)
    lon_lf, lon_rt = lax.rem(lon + n_lon - 1, n_lon), lax.rem(lon + 1, n_lon)

    barrier = pltpu.get_barrier_semaphore()
    peers = [(sib, lon)]
    peers += [(lat, at_x(d)) for d in range(1, NX)] + [(sib, at_x(d)) for d in range(1, NX)]
    peers += [(lat, at_y(d)) for d in range(1, NY)] + [(at_z(d), lon) for d in range(1, NZ)]
    peers += [
        (a, b)
        for a in (lat_up, lat, lat_dn)
        for b in (lon_lf, lon, lon_rt)
        if not (a is lat and b is lon)
    ]
    for peer in peers:
        pl.semaphore_signal(barrier, inc=1, device_id=peer, device_id_type=pl.DeviceIdType.MESH)

    half = pl.ds(pl.multiple_of(core * 128, 128), 128)
    loads = []

    def load(src, dst):
        copy = pltpu.make_async_copy(src, dst, load_sem.at[len(loads)])
        copy.start()
        loads.append(copy)

    load(w1_ref.at[:, :, half], wl.at[0, core, x, y])
    load(act_ref, xs.at[0, OWN : OWN + CELLS])
    load(basis_ref, basis)
    load(depth_ref, depth)
    load(extent_ref, extent)
    load(w2_ref.at[:, :, half], wl.at[1, core, x, y])
    load(cot_ref, cot)

    sent = []

    def send(copies, whole):
        slot = len(sent)

        def describe(src, dst, device):
            return pltpu.make_async_remote_copy(
                src_ref=src,
                dst_ref=dst,
                send_sem=send_sem.at[slot],
                recv_sem=recv_sem.at[slot],
                device_id=device,
                device_id_type=pl.DeviceIdType.MESH,
            )

        for src, dst, device in copies:
            describe(src, dst, device).start()
        group = describe(whole, whole, (sib, lon))
        sent.append(group)
        return group, describe

    def arrive(group):
        for copy in group[:1]:
            copy.wait_recv()

    xs[:, 3 * SIDE : EXT, :] = jnp.zeros((4, EXT - 3 * SIDE, CH), BF16)
    loads[0].wait()
    loads[1].wait()
    pl.semaphore_wait(barrier, len(peers))

    def halo(n):
        own = xs.at[n, OWN : OWN + CELLS]
        top = xs.at[n, OWN : OWN + 16]
        bottom = xs.at[n, OWN + CELLS - 16 : OWN + CELLS]
        lf, mid, rt = 0, SIDE, 2 * SIDE
        low, high = 16, SIDE - 16

        def to(src, base, off, rows, device):
            return src, xs.at[n, base + off : base + off + rows], device

        return send(
            [
                to(own, lf, low, CELLS, (lat, lon_rt)),
                to(own, rt, low, CELLS, (lat, lon_lf)),
                to(bottom, lf, 0, 16, (lat_dn, lon_rt)),
                to(bottom, rt, 0, 16, (lat_dn, lon_lf)),
                to(top, lf, high, 16, (lat_up, lon_rt)),
                to(top, rt, high, 16, (lat_up, lon_lf)),
                to(bottom, mid, 0, 16, (lat_dn, lon)),
                to(top, mid, high, 16, (lat_up, lon)),
            ],
            xs.at[n, 0 : 2 * CELLS + 6 * 16],
        )

    def gather(w):
        ka, kc = slice(0, SPLIT), slice(SPLIT, BASIS)
        mine_a, mine_c = wl.at[w, core, x, y, ka], wl.at[w, core, x, y, kc]
        first_c = send(
            [(mine_c, mine_c, (lat, at_y(d))) for d in range(1, NY)], wl.at[w, core, x, 0 : NY - 1, kc]
        )
        first_a = send(
            [(mine_a, mine_a, (lat, at_x(d))) for d in range(1, NX)], wl.at[w, core, 0 : NX - 1, y, ka]
        )
        yield
        arrive(first_a)
        column = wl.at[w, core, :, y, ka]
        second_a = send(
            [(column, column, (lat, at_y(d))) for d in range(1, NY)], wl.at[w, core, :, 0 : NY - 1, ka]
        )
        arrive(first_c)

        def row(d):
            return wl.at[w, core, lax.rem(x + d, NX), :, kc]

        second_c = [send([(row(0), row(0), (lat, at_x(d)))], row(0)) for d in range(1, NX)]
        whole = wl.at[w, core]
        shared = send([(row(0), row(0), (sib, lon))], whole)

        def share(ref):
            shared[1](ref, ref, (sib, lon)).start()

        yield
        for d in (1, 3, 2):
            arrive(second_c[d - 1])
            share(row(NX - d))
        arrive(second_a)
        share(wl.at[w, core, :, :, ka])
        yield
        arrive(shared)

    gather1, gather2 = gather(0), gather(1)
    next(gather1)
    in_halo = halo(0)

    for copy in loads[2:5]:
        copy.wait()
    sub = lax.broadcasted_iota(jnp.int32, (8, 128), 0)
    lane = lax.broadcasted_iota(jnp.int32, (8, 128), 1)
    slot_a = (lane * 2731) >> 16
    slot_b = lane - 24 * slot_a
    row0 = lat * ROWS
    picks = 8 * (ROWS + 4)
    pick_row = lax.broadcasted_iota(jnp.int32, (picks, GRID), 0) >> 3
    pick_lane = lax.broadcasted_iota(jnp.int32, (picks, GRID), 1)
    pick = jnp.where(pick_lane == pick_row + row0 - 2, 1.0, 0.0).astype(BF16)
    for k in range(BASIS):
        for a in range(5):
            pad[k, 24 * a : 24 * a + 17, :] = basis[k, a].astype(F32)
        picked = lax.dot_general(
            pick, pad[k].astype(BF16), (((1,), (1,)), ((), ())), preferred_element_type=F32
        )
        cb[:, k] = picked.reshape(ROWS + 4, 8, 128)

    def coef_row(r, carry):
        wrapped = lax.rem(row0 + r + GRID - 2, GRID)
        inside = (
            (jnp.abs(slot_a - 2) <= depth[wrapped])
            & (jnp.abs(slot_b - 8) <= extent[wrapped])
            & (slot_a < 5)
        )
        for k in range(BASIS):
            cb[r, k] = jnp.where(inside, cb[r, k], 0.0)
        return carry

    lax.fori_loop(0, ROWS + 4, coef_row, 0)

    wide_l = lax.broadcasted_iota(jnp.int32, (256, EXT), 0)
    wide_t = lax.broadcasted_iota(jnp.int32, (256, EXT), 1)
    l_q = wide_l >> 7
    l_in = wide_l & 127
    l_a = (l_in * 2731) >> 16
    l_m = l_in - 24 * l_a

    def build(n):
        def pair(p, carry):
            for q in range(2):
                i = 2 * p + q
                row = row0 + i
                for k in range(BASIS):
                    if n == 0:
                        reach = row + slot_a - 2
                        tile = jnp.where((reach >= 0) & (reach < GRID), cb[i + 2, k], 0.0)
                        tile = pltpu.roll(tile, 0, 1, stride=1, stride_axis=0)
                    else:
                        tile = cb[i + 4, k]
                        for a in range(1, 5):
                            tile = jnp.where(slot_a == a, cb[i + 4 - a, k], tile)
                        tile = pltpu.roll(tile, 0, 1, stride=1, stride_axis=0)
                    t1[p, k, 8 * q : 8 * q + 8, 128 * q : 128 * q + 128] = tile
                    t1[p, k, 8 * q : 8 * q + 8, 128 * (1 - q) : 128 * (1 - q) + 128] = jnp.zeros(
                        (8, 128), F32
                    )
            return carry

        if n == 1:
            src = lax.broadcasted_iota(jnp.int32, (128, 128), 0)
            dst = lax.broadcasted_iota(jnp.int32, (128, 128), 1)
            src_a = (src * 2731) >> 16
            mirror = jnp.where(
                (dst == 48 * src_a + 16 - src) & (src - 24 * src_a < 17) & (src_a < 5), 1.0, 0.0
            ).astype(BF16)
            for r in range(0, ROWS + 4, 4):
                rows = cb[r : r + 4].reshape(4 * BASIS * 8, 128).astype(BF16)
                cb[r : r + 4] = jnp.dot(rows, mirror, preferred_element_type=F32).reshape(
                    4, BASIS, 8, 128
                )
        lax.fori_loop(0, 8, pair, 0)
        m = l_m
        shift = l_q + (l_a if n == 0 else 4 - l_a)
        place = jnp.where(
            (wide_t == (m >> 3) * SIDE + 8 * shift + (m & 7)) & (l_a < 5), 1.0, 0.0
        ).astype(BF16)
        for p in range(8):
            spread = jnp.dot(
                t1[p].reshape(16 * BASIS, 256).astype(BF16), place, preferred_element_type=F32
            )
            spread = pltpu.roll(spread, 16 * p, 1) if p else spread
            tmap[n, :, 16 * p : 16 * p + 16, :] = spread.reshape(BASIS, 16, EXT).astype(BF16)

    build(0)

    def conv(n, field):
        for k in range(0, BASIS, 3):
            part = jnp.dot(
                tmap[n, k : k + 3].reshape(3 * CELLS, EXT), xs[field], preferred_element_type=F32
            )
            zb[k : k + 3] = part.astype(BF16).reshape(3, CELLS, CH)

    def spread_z(layer):
        for k in range(BASIS):
            zt[layer, k] = zb[k].astype(F32).T.astype(BF16)

        def block(d):
            return zt.at[layer, :, pl.ds(lax.rem(x + d, NX) * 64, 64)]

        zg[layer, x, core] = zt[layer, :, pl.ds(pl.multiple_of(x * 64, 64), 64)]
        got = send(
            [(block(d), zg.at[layer, x, core], (lat, at_x(d))) for d in range(1, NX)],
            zg.at[layer, 0 : NX - 1, core],
        )
        yield
        arrive(got)
        mine = zg.at[layer, :, core]
        shared = send([(mine, mine, (sib, lon))], mine)
        yield
        arrive(shared)

    def settle(w):
        for k in range(BASIS):
            for h in range(2):
                wf[w, k, :, h * 128 : (h + 1) * 128] = (
                    wl[w, h, :, :, k].astype(F32).reshape(CH, 128).astype(BF16)
                )

    def mix(w):
        total = jnp.zeros((CELLS, CH), F32)
        for k in range(BASIS):
            total += jnp.dot(zb[k], wf[w, k], preferred_element_type=F32)
        return total

    def mix_back(w):
        total = jnp.zeros((CELLS, CH), F32)
        for k in range(BASIS):
            total += lax.dot_general(
                zb[k], wf[w, k], (((1,), (1,)), ((), ())), preferred_element_type=F32
            )
        return total

    def own_block(n):
        return xs[n, OWN : OWN + CELLS, :].astype(F32)

    def spread_s(layer, n, values):
        xs[n, OWN : OWN + CELLS, :] = values
        around = halo(n)
        for h in range(2):

            @pl.when(core == h)
            def _():
                sg[layer, x, h] = values[:, h * 128 : (h + 1) * 128]

        copies = []
        for d in (1, 3, 2, 0):
            for dc in range(2):
                if d == 0 and dc == 0:
                    continue
                h = core if dc == 0 else other
                src = xs.at[n, OWN : OWN + CELLS, pl.ds(pl.multiple_of(h * 128, 128), 128)]
                copies.append((src, sg.at[layer, x, core], (lat if dc == 0 else sib, at_x(d))))
        return around, send(copies, xs.at[n, 0 : 7 * CELLS // 2])

    def weight_partial(layer):
        groups = []
        for c in range(PARTS):
            total = jnp.zeros((DEEP * 64, 128), F32)
            ks = slice(DEEP * c, DEEP * c + DEEP)
            for a in range(NX):
                left = jnp.concatenate(
                    [zg[layer, a, h, ks].reshape(DEEP * 64, 128) for h in range(2)], axis=1
                )
                total += jnp.dot(left, sg[layer, a].reshape(256, 128), preferred_element_type=F32)
            blocks = total.reshape(DEEP, NY, 8, 128)
            for b in range(NY):
                pb[layer, c, b] = blocks[:, b].astype(BF16)
            ry[layer, c, y] = pb[layer, c, y]
            groups.append(
                send(
                    [
                        (pb.at[layer, c, lax.rem(y + d, NY)], ry.at[layer, c, y], (lat, at_y(d)))
                        for d in (4, 3, 5, 2, 6, 1, 7)
                    ],
                    ry.at[layer, c, 0 : NY - 1],
                )
            )
        return groups

    def weight_rows(layer, got):
        groups = []
        for c in range(PARTS):
            arrive(got[c])
            qy[layer, c] = jnp.sum(ry[layer, c].astype(F32), axis=0).astype(BF16)
            rz[layer, c, z] = qy[layer, c]
            groups.append(
                send(
                    [
                        (qy.at[layer, c], rz.at[layer, c, z], (at_z(d), lon))
                        for d in (4, 3, 5, 2, 6, 1, 7)
                    ],
                    rz.at[layer, c, 0 : NZ - 1],
                )
            )
        return groups

    def weight_bands(layer, got):
        groups = []
        for c in range(PARTS):
            arrive(got[c])
            ks = slice(DEEP * c, DEEP * c + DEEP)
            fin[layer, core, ks] = jnp.sum(rz[layer, c].astype(F32), axis=0)
            mine = fin.at[layer, core, ks]
            groups.append(send([(mine, mine, (sib, lon))], mine))
        return groups

    next(gather1)
    loads[5].wait()
    next(gather2)
    build(1)
    arrive(in_halo)
    conv(0, 0)
    next(gather2)
    next(gather1)
    next(gather1, None)
    settle(0)
    y1 = mix(0)
    yb[...] = y1
    hidden = (own_block(0) + gelu_and_slope(y1)[0]).astype(BF16)
    xs[1, OWN : OWN + CELLS, :] = hidden
    mid_halo = halo(1)
    z1 = spread_z(0)
    next(z1)
    next(gather2)
    next(gather2, None)
    settle(1)
    arrive(mid_halo)
    conv(0, 1)
    y2 = mix(1)
    grown, slope = gelu_and_slope(y2)
    loads[6].wait()
    around2, all_s2 = spread_s(1, 2, (cot[...].astype(F32) * slope).astype(BF16))
    out_ref[...] = (own_block(1) + grown).astype(BF16)
    z2 = spread_z(1)
    next(z2)
    next(z1)
    arrive(around2)
    conv(1, 2)
    grad_hidden = (cot[...].astype(F32) + mix_back(1)).astype(BF16).astype(F32)
    s1 = (grad_hidden * gelu_and_slope(yb[...])[1]).astype(BF16)
    around1, all_s1 = spread_s(0, 3, s1)
    next(z2)
    arrive(all_s2)
    next(z1, None)
    next(z2, None)
    p2 = weight_partial(1)
    arrive(all_s1)
    p1 = weight_partial(0)
    arrive(around1)
    conv(1, 3)
    q2 = weight_rows(1, p2)
    gfield_ref[...] = (grad_hidden + mix_back(0)).astype(BF16)
    q1 = weight_rows(0, p1)
    r2 = weight_bands(1, q2)
    r1 = weight_bands(0, q1)
    for layer, ref, got in ((1, g2_ref, r2), (0, g1_ref, r1)):
        for group in got:
            arrive(group)
        for h in range(2):
            ref[:, :, h * 128 : (h + 1) * 128] = fin[layer, h]
    for copy in sent:
        copy.wait_send()


def deliver(*refs):
    count = len(refs) // 2
    for src, dst in zip(refs[:count], refs[count:]):
        dst[...] = src[...]


def local(activation, basis_table, lat_depth, lon_extent, weight_one, weight_two, cotangent):
    vmem = pl.BlockSpec(memory_space=pltpu.VMEM)
    hbm = pl.BlockSpec(memory_space=pltpu.HBM)
    field = jax.ShapeDtypeStruct((CELLS, CH), BF16)
    grad = jax.ShapeDtypeStruct((BASIS, 8, CH), F32)
    shapes = (field, field, grad, grad)
    results = pl.pallas_call(
        kernel,
        out_shape=shapes,
        in_specs=[hbm] * 7,
        out_specs=(vmem,) * 4,
        scratch_shapes=[
            pltpu.VMEM((BASIS, 5, 17, GRID), BF16),
            pltpu.SMEM((GRID,), jnp.int32),
            pltpu.SMEM((GRID,), jnp.int32),
            pltpu.VMEM((CELLS, CH), BF16),
            pltpu.VMEM((BASIS, 128, GRID), F32),
            pltpu.VMEM((ROWS + 4, BASIS, 8, 128), F32),
            pltpu.VMEM((8, BASIS, 16, 256), F32),
            pltpu.VMEM((2, BASIS, CELLS, EXT), BF16),
            pltpu.VMEM((4, EXT, CH), BF16),
            pltpu.VMEM((2, 2, NX, NY, BASIS, 8, 128), BF16),
            pltpu.VMEM((2, BASIS, CH, CH), BF16),
            pltpu.VMEM((BASIS, CELLS, CH), BF16),
            pltpu.VMEM((2, BASIS, CH, CELLS), BF16),
            pltpu.VMEM((2, NX, 2, BASIS, 64, CELLS), BF16),
            pltpu.VMEM((2, NX, 2, CELLS, 128), BF16),
            pltpu.VMEM((2, PARTS, NY, DEEP, 8, 128), BF16),
            pltpu.VMEM((2, PARTS, NY, DEEP, 8, 128), BF16),
            pltpu.VMEM((2, PARTS, DEEP, 8, 128), BF16),
            pltpu.VMEM((2, PARTS, NZ, DEEP, 8, 128), BF16),
            pltpu.VMEM((2, 2, BASIS, 8, 128), F32),
            pltpu.VMEM((CELLS, CH), F32),
            pltpu.SemaphoreType.DMA((SLOTS,)),
            pltpu.SemaphoreType.DMA((SLOTS,)),
            pltpu.SemaphoreType.DMA((7,)),
        ],
        compiler_params=pltpu.CompilerParams(
            collective_id=0, has_side_effects=True, vmem_limit_bytes=63 * 1024 * 1024
        ),
        cost_estimate=pl.CostEstimate(flops=10**9, bytes_accessed=10**7, transcendentals=10**5),
    )(
        activation.reshape(CELLS, CH),
        jnp.transpose(basis_table, (0, 2, 3, 1)),
        lat_depth,
        lon_extent,
        weight_one,
        weight_two,
        cotangent.reshape(CELLS, CH),
    )
    out, grad_field, grad_one, grad_two = pl.pallas_call(
        deliver,
        out_shape=shapes,
        in_specs=[vmem] * 4,
        out_specs=(vmem,) * 4,
    )(*results)
    block = (ROWS, COLS, CH)
    return out.reshape(block), grad_field.reshape(block), grad_one, grad_two


def solution(mesh):
    field = P("lat", "lon", None)
    weight = P(None, "lon", None)
    return jax.shard_map(
        local,
        mesh=mesh,
        in_specs=(field, P(), P(), P(), weight, weight, field),
        out_specs=(field, field, weight, weight),
        check_vma=False,
    )
```

time: 104 us -> 74.9 us (0.72)
  Pallas kernels: 92.5 us -> 74.1 us
  local copies, waits for them, and re-layouts: 9.99 us -> 0 us
    pallas_call x1 -> x2, Pallas kernels: 92.5 us -> 74.1 us  [the longest x1 72.4 us: local(): pl.pallas_call(kernel, out_shape=shapes, in_specs=[hbm] * 7, out_specs=(v...]
    unnamed x19 -> x0, local copies, waits for them, and re-layouts: 9.99 us -> none
where the time goes in v2:
time: 74.9 us; the launch traced here: 74.7 us
  Pallas kernels  74.1 us (99%)
    pallas_call x1, Pallas kernels, local(): pl.pallas_call(kernel, out_shape=shapes, in_specs=[hbm] * 7, out_specs=(v...  72.4 us
    pallas_call x1, Pallas kernels, local(): pl.pallas_call(deliver, out_shape=shapes, in_specs=[vmem] * 4, out_specs=...  1.7 us

profile of v2, /device:TPU:1, one launch (start us, length us, event | category | flops | bytes accessed | tf_op | source)
XLA Modules:
  0.0 74.7 jit_solution(10628847382083162723)
XLA Ops:
  0.6 72.4 %shard_map.102 = (bf16[128,256]{1,0:T(8,128)(2,1)}, bf16[128,256]{1,0:T(8,128)(2,1)}, f32[9,8,256]{2,1,0:T(8,128)}, f32[9,8,256]{2,1,0:T(8,128)}) custom-call(bf16[128,256]{1,0:T(8,128)(2,1)} %bitcast.6, bf16[9,5,17,256]{3,2,1,0:T(8,128)(2,1)} %bitcast.5, s32[256]{0:T(256)} %depth_ref.1, s32[256]{0:T(256)} %extent_ref.1, bf16[9,8,256]{2,1,0:T(8,128)(2,1)} %w1_ref.1, ...), custom_call_target="tpu_custom_call" | custom-call | flops 1000000000 | bytes 10000000 | tf_op jit(solution)/shard_map/pallas_call | solution.py:490
  73.0 1.7 %shard_map.103 = (bf16[128,256]{1,0:T(8,128)(2,1)}, bf16[128,256]{1,0:T(8,128)(2,1)}, f32[9,8,256]{2,1,0:T(8,128)}, f32[9,8,256]{2,1,0:T(8,128)}) custom-call(bf16[128,256]{1,0:T(8,128)(2,1)} %get-tuple-element.12.refs_0_, bf16[128,256]{1,0:T(8,128)(2,1)} %get-tuple-element.13.refs_1_, f32[9,8,256]{2,1,0:T(8,128)} %get-tuple-element.14.refs_2_, ...), custom_call_target="tpu_custom_call" | custom-call | tf_op jit(solution)/shard_map/pallas_call | solution.py:534

commit v3 on v2

--- a/solution.py
+++ b/solution.py
@@ -16,7 +16,7 @@
 OWN = SIDE + 2 * COLS
 F32 = jnp.float32
 BF16 = jnp.bfloat16
-SLOTS = 48
+SLOTS = 60
 SPLIT = 2
 PARTS, DEEP = 3, 3
 
@@ -53,7 +53,8 @@
     wl,
     wf,
     zb,
-    zt,
+    xt,
+    xg,
     zg,
     sg,
     pb,
@@ -134,10 +135,10 @@
             describe(src, dst, device).start()
         group = describe(whole, whole, (sib, lon))
         sent.append(group)
-        return group, describe
-
-    def arrive(group):
-        for copy in group[:1]:
+        return group
+
+    def arrive(*groups):
+        for copy in groups:
             copy.wait_recv()
 
     xs[:, 3 * SIDE : EXT, :] = jnp.zeros((4, EXT - 3 * SIDE, CH), BF16)
@@ -190,12 +191,12 @@
             return wl.at[w, core, lax.rem(x + d, NX), :, kc]
 
         second_c = [send([(row(0), row(0), (lat, at_x(d)))], row(0)) for d in range(1, NX)]
-        whole = wl.at[w, core]
-        shared = send([(row(0), row(0), (sib, lon))], whole)
+        shared = []
 
         def share(ref):
-            shared[1](ref, ref, (sib, lon)).start()
-
+            shared.append(send([(ref, ref, (sib, lon))], ref))
+
+        share(row(0))
         yield
         for d in (1, 3, 2):
             arrive(second_c[d - 1])
@@ -203,11 +204,13 @@
         arrive(second_a)
         share(wl.at[w, core, :, :, ka])
         yield
-        arrive(shared)
+        arrive(*shared)
 
     gather1, gather2 = gather(0), gather(1)
     next(gather1)
     in_halo = halo(0)
+    loads[5].wait()
+    next(gather2)
 
     for copy in loads[2:5]:
         copy.wait()
@@ -303,20 +306,31 @@
             )
             zb[k : k + 3] = part.astype(BF16).reshape(3, CELLS, CH)
 
-    def spread_z(layer):
-        for k in range(BASIS):
-            zt[layer, k] = zb[k].astype(F32).T.astype(BF16)
+    def spread_x(layer):
+        xt[layer] = xs[layer].astype(F32).T.astype(BF16)
+        xg[layer, x] = xt[layer, pl.ds(pl.multiple_of(x * 64, 64), 64)]
 
         def block(d):
-            return zt.at[layer, :, pl.ds(lax.rem(x + d, NX) * 64, 64)]
-
-        zg[layer, x, core] = zt[layer, :, pl.ds(pl.multiple_of(x * 64, 64), 64)]
+            return xt.at[layer, pl.ds(pl.multiple_of(lax.rem(x + d, NX) * 64, 64), 64)]
+
         got = send(
-            [(block(d), zg.at[layer, x, core], (lat, at_x(d))) for d in range(1, NX)],
-            zg.at[layer, 0 : NX - 1, core],
+            [(block(d), xg.at[layer, x], (lat, at_x(d))) for d in (2, 1, 3)],
+            xg.at[layer, 0 : NX - 1],
         )
         yield
         arrive(got)
+        for k in range(0, BASIS, 3):
+            part = lax.dot_general(
+                xg[layer].reshape(NX * 64, EXT),
+                tmap[0, k : k + 3].reshape(3 * CELLS, EXT),
+                (((1,), (1,)), ((), ())),
+                preferred_element_type=F32,
+            ).astype(BF16)
+            for a in range(NX):
+                for b in range(3):
+                    zg[layer, a, core, k + b] = part[
+                        64 * a : 64 * a + 64, CELLS * b : CELLS * b + CELLS
+                    ]
         mine = zg.at[layer, :, core]
         shared = send([(mine, mine, (sib, lon))], mine)
         yield
@@ -348,7 +362,8 @@
 
     def spread_s(layer, n, values):
         xs[n, OWN : OWN + CELLS, :] = values
-        around = halo(n)
+        if layer:
+            around = halo(n)
         for h in range(2):
 
             @pl.when(core == h)
@@ -363,7 +378,10 @@
                 h = core if dc == 0 else other
                 src = xs.at[n, OWN : OWN + CELLS, pl.ds(pl.multiple_of(h * 128, 128), 128)]
                 copies.append((src, sg.at[layer, x, core], (lat if dc == 0 else sib, at_x(d))))
-        return around, send(copies, xs.at[n, 0 : 7 * CELLS // 2])
+        spread = send(copies, xs.at[n, 0 : 7 * CELLS // 2])
+        if not layer:
+            around = halo(n)
+        return around, spread
 
     def weight_partial(layer):
         groups = []
@@ -418,12 +436,10 @@
         return groups
 
     next(gather1)
-    loads[5].wait()
+    build(1)
     next(gather2)
-    build(1)
     arrive(in_halo)
     conv(0, 0)
-    next(gather2)
     next(gather1)
     next(gather1, None)
     settle(0)
@@ -432,27 +448,27 @@
     hidden = (own_block(0) + gelu_and_slope(y1)[0]).astype(BF16)
     xs[1, OWN : OWN + CELLS, :] = hidden
     mid_halo = halo(1)
-    z1 = spread_z(0)
+    z1 = spread_x(0)
     next(z1)
     next(gather2)
     next(gather2, None)
     settle(1)
+    next(z1)
     arrive(mid_halo)
     conv(0, 1)
+    z2 = spread_x(1)
+    next(z2)
     y2 = mix(1)
     grown, slope = gelu_and_slope(y2)
     loads[6].wait()
     around2, all_s2 = spread_s(1, 2, (cot[...].astype(F32) * slope).astype(BF16))
     out_ref[...] = (own_block(1) + grown).astype(BF16)
-    z2 = spread_z(1)
     next(z2)
-    next(z1)
     arrive(around2)
     conv(1, 2)
     grad_hidden = (cot[...].astype(F32) + mix_back(1)).astype(BF16).astype(F32)
     s1 = (grad_hidden * gelu_and_slope(yb[...])[1]).astype(BF16)
     around1, all_s1 = spread_s(0, 3, s1)
-    next(z2)
     arrive(all_s2)
     next(z1, None)
     next(z2, None)
@@ -505,7 +521,8 @@
             pltpu.VMEM((2, 2, NX, NY, BASIS, 8, 128), BF16),
             pltpu.VMEM((2, BASIS, CH, CH), BF16),
             pltpu.VMEM((BASIS, CELLS, CH), BF16),
-            pltpu.VMEM((2, BASIS, CH, CELLS), BF16),
+            pltpu.VMEM((2, CH, EXT), BF16),
+            pltpu.VMEM((2, NX, 64, EXT), BF16),
             pltpu.VMEM((2, NX, 2, BASIS, 64, CELLS), BF16),
             pltpu.VMEM((2, NX, 2, CELLS, 128), BF16),
             pltpu.VMEM((2, PARTS, NY, DEEP, 8, 128), BF16),

time: 74.9 us -> 69.4 us (0.927)
  Pallas kernels: 74.1 us -> 68.6 us
    pallas_call x1, Pallas kernels: 72.4 us -> 66.9 us  [local(): pl.pallas_call(kernel, out_shape=shapes, in_specs=[hbm] * 7, out_specs=(v...]
where the time goes in v3:
time: 69.4 us; the launch traced here: 69.2 us
  Pallas kernels  68.6 us (99%)
    pallas_call x1, Pallas kernels, local(): pl.pallas_call(kernel, out_shape=shapes, in_specs=[hbm] * 7, out_specs=(v...  66.9 us
    pallas_call x1, Pallas kernels, local(): pl.pallas_call(deliver, out_shape=shapes, in_specs=[vmem] * 4, out_specs=...  1.7 us

profile of v3, /device:TPU:1, one launch (start us, length us, event | category | flops | bytes accessed | tf_op | source)
XLA Modules:
  0.0 69.2 jit_solution(12765009006194157228)
XLA Ops:
  0.6 66.9 %shard_map.102 = (bf16[128,256]{1,0:T(8,128)(2,1)}, bf16[128,256]{1,0:T(8,128)(2,1)}, f32[9,8,256]{2,1,0:T(8,128)}, f32[9,8,256]{2,1,0:T(8,128)}) custom-call(bf16[128,256]{1,0:T(8,128)(2,1)} %bitcast.6, bf16[9,5,17,256]{3,2,1,0:T(8,128)(2,1)} %bitcast.5, s32[256]{0:T(256)} %depth_ref.1, s32[256]{0:T(256)} %extent_ref.1, bf16[9,8,256]{2,1,0:T(8,128)(2,1)} %w1_ref.1, ...), custom_call_target="tpu_custom_call" | custom-call | flops 1000000000 | bytes 10000000 | tf_op jit(solution)/shard_map/pallas_call | solution.py:506
  67.5 1.7 %shard_map.103 = (bf16[128,256]{1,0:T(8,128)(2,1)}, bf16[128,256]{1,0:T(8,128)(2,1)}, f32[9,8,256]{2,1,0:T(8,128)}, f32[9,8,256]{2,1,0:T(8,128)}) custom-call(bf16[128,256]{1,0:T(8,128)(2,1)} %get-tuple-element.12.refs_0_, bf16[128,256]{1,0:T(8,128)(2,1)} %get-tuple-element.13.refs_1_, f32[9,8,256]{2,1,0:T(8,128)} %get-tuple-element.14.refs_2_, ...), custom_call_target="tpu_custom_call" | custom-call | tf_op jit(solution)/shard_map/pallas_call | solution.py:551

commit v4 on v3

--- a/solution.py
+++ b/solution.py
@@ -11,13 +11,15 @@
 ROWS, COLS = 16, 8
 CELLS = ROWS * COLS
 GRID = 256
-SIDE = (ROWS + 4) * COLS
-EXT = 512
-OWN = SIDE + 2 * COLS
+SIDE = (ROWS + 8) * COLS
+EXT = 640
+OWN = SIDE + 4 * COLS
+WIDE = (ROWS + 4) * COLS
+FIRST = 1024
 F32 = jnp.float32
 BF16 = jnp.bfloat16
 SLOTS = 60
-SPLIT = 2
+SPLIT = 1
 PARTS, DEEP = 3, 3
 
 
@@ -48,11 +50,14 @@
     pad,
     cb,
     t1,
-    tmap,
+    tfwd,
+    tadj,
+    first,
     xs,
     wl,
     wf,
     zb,
+    zw,
     xt,
     xg,
     zg,
@@ -85,18 +90,18 @@
 
     n_lat, n_lon = 2 * NZ, NX * NY
     lat_up, lat_dn = lax.rem(lat + n_lat - 1, n_lat), lax.rem(lat + 1, n_lat)
-    lon_lf, lon_rt = lax.rem(lon + n_lon - 1, n_lon), lax.rem(lon + 1, n_lon)
+
+    def at_lon(d):
+        return lax.rem(lon + d + n_lon, n_lon)
+
+    lon_lf, lon_rt = at_lon(-1), at_lon(1)
 
     barrier = pltpu.get_barrier_semaphore()
     peers = [(sib, lon)]
     peers += [(lat, at_x(d)) for d in range(1, NX)] + [(sib, at_x(d)) for d in range(1, NX)]
     peers += [(lat, at_y(d)) for d in range(1, NY)] + [(at_z(d), lon) for d in range(1, NZ)]
-    peers += [
-        (a, b)
-        for a in (lat_up, lat, lat_dn)
-        for b in (lon_lf, lon, lon_rt)
-        if not (a is lat and b is lon)
-    ]
+    peers += [(a, at_lon(d)) for a in (lat_up, lat_dn) for d in (-2, -1, 0, 1, 2)]
+    peers += [(lat, at_lon(d)) for d in (-2, -1, 1, 2)]
     for peer in peers:
         pl.semaphore_signal(barrier, inc=1, device_id=peer, device_id_type=pl.DeviceIdType.MESH)
 
@@ -109,7 +114,7 @@
         loads.append(copy)
 
     load(w1_ref.at[:, :, half], wl.at[0, core, x, y])
-    load(act_ref, xs.at[0, OWN : OWN + CELLS])
+    load(act_ref, first.at[SIDE + OWN : SIDE + OWN + CELLS])
     load(basis_ref, basis)
     load(depth_ref, depth)
     load(extent_ref, extent)
@@ -141,17 +146,22 @@
         for copy in groups:
             copy.wait_recv()
 
-    xs[:, 3 * SIDE : EXT, :] = jnp.zeros((4, EXT - 3 * SIDE, CH), BF16)
+    first[5 * SIDE : FIRST, :] = jnp.zeros((FIRST - 5 * SIDE, CH), BF16)
+    for side in range(3):
+        for edge in (side * SIDE, side * SIDE + SIDE - 16):
+            xs[:, edge : edge + 16, :] = jnp.zeros((3, 16, CH), BF16)
+    xs[:, 3 * SIDE : EXT, :] = jnp.zeros((3, EXT - 3 * SIDE, CH), BF16)
     loads[0].wait()
     loads[1].wait()
     pl.semaphore_wait(barrier, len(peers))
 
-    def halo(n):
+    def halo(field):
+        n = field - 1
         own = xs.at[n, OWN : OWN + CELLS]
         top = xs.at[n, OWN : OWN + 16]
         bottom = xs.at[n, OWN + CELLS - 16 : OWN + CELLS]
         lf, mid, rt = 0, SIDE, 2 * SIDE
-        low, high = 16, SIDE - 16
+        low, high = 32, SIDE - 32
 
         def to(src, base, off, rows, device):
             return src, xs.at[n, base + off : base + off + rows], device
@@ -160,15 +170,28 @@
             [
                 to(own, lf, low, CELLS, (lat, lon_rt)),
                 to(own, rt, low, CELLS, (lat, lon_lf)),
-                to(bottom, lf, 0, 16, (lat_dn, lon_rt)),
-                to(bottom, rt, 0, 16, (lat_dn, lon_lf)),
+                to(bottom, lf, 16, 16, (lat_dn, lon_rt)),
+                to(bottom, rt, 16, 16, (lat_dn, lon_lf)),
                 to(top, lf, high, 16, (lat_up, lon_rt)),
                 to(top, rt, high, 16, (lat_up, lon_lf)),
-                to(bottom, mid, 0, 16, (lat_dn, lon)),
+                to(bottom, mid, 16, 16, (lat_dn, lon)),
                 to(top, mid, high, 16, (lat_up, lon)),
             ],
             xs.at[n, 0 : 2 * CELLS + 6 * 16],
         )
+
+    def wide_halo():
+        base = SIDE + OWN
+        own = first.at[base : base + CELLS]
+        top, bottom = first.at[base : base + 32], first.at[base + CELLS - 32 : base + CELLS]
+        copies = []
+        for d in (-1, 1, -2, 2, 0):
+            at = (2 - d) * SIDE
+            copies.append((bottom, first.at[at : at + 32], (lat_dn, at_lon(d))))
+            copies.append((top, first.at[at + SIDE - 32 : at + SIDE], (lat_up, at_lon(d))))
+            if d:
+                copies.append((own, first.at[at + 32 : at + 32 + CELLS], (lat, at_lon(d))))
+        return send(copies, first.at[0 : 4 * CELLS + 10 * 32])
 
     def gather(w):
         ka, kc = slice(0, SPLIT), slice(SPLIT, BASIS)
@@ -208,7 +231,7 @@
 
     gather1, gather2 = gather(0), gather(1)
     next(gather1)
-    in_halo = halo(0)
+    in_halo = wide_halo()
     loads[5].wait()
     next(gather2)
 
@@ -255,11 +278,11 @@
         def pair(p, carry):
             for q in range(2):
                 i = 2 * p + q
-                row = row0 + i
+                row = row0 + i - 2
                 for k in range(BASIS):
                     if n == 0:
                         reach = row + slot_a - 2
-                        tile = jnp.where((reach >= 0) & (reach < GRID), cb[i + 2, k], 0.0)
+                        tile = jnp.where((reach >= 0) & (reach < GRID), cb[i, k], 0.0)
                         tile = pltpu.roll(tile, 0, 1, stride=1, stride_axis=0)
                     else:
                         tile = cb[i + 4, k]
@@ -284,30 +307,54 @@
                 cb[r : r + 4] = jnp.dot(rows, mirror, preferred_element_type=F32).reshape(
                     4, BASIS, 8, 128
                 )
-        lax.fori_loop(0, 8, pair, 0)
+        pairs = 8 if n else 10
+        lax.fori_loop(0, pairs, pair, 0)
         m = l_m
-        shift = l_q + (l_a if n == 0 else 4 - l_a)
+        shift = l_q + (l_a if n == 0 else 6 - l_a)
         place = jnp.where(
             (wide_t == (m >> 3) * SIDE + 8 * shift + (m & 7)) & (l_a < 5), 1.0, 0.0
         ).astype(BF16)
-        for p in range(8):
+        for p in range(pairs):
             spread = jnp.dot(
                 t1[p].reshape(16 * BASIS, 256).astype(BF16), place, preferred_element_type=F32
             )
             spread = pltpu.roll(spread, 16 * p, 1) if p else spread
-            tmap[n, :, 16 * p : 16 * p + 16, :] = spread.reshape(BASIS, 16, EXT).astype(BF16)
+            (tadj if n else tfwd)[:, 16 * p : 16 * p + 16, :] = spread.reshape(BASIS, 16, EXT).astype(BF16)
 
     build(0)
 
     def conv(n, field):
         for k in range(0, BASIS, 3):
+            maps = tadj[k : k + 3] if n else tfwd[k : k + 3, 16 : 16 + CELLS]
             part = jnp.dot(
-                tmap[n, k : k + 3].reshape(3 * CELLS, EXT), xs[field], preferred_element_type=F32
+                maps.reshape(3 * CELLS, EXT), xs[field - 1], preferred_element_type=F32
             )
             zb[k : k + 3] = part.astype(BF16).reshape(3, CELLS, CH)
 
+    def conv_wide():
+        for side in range(3):
+            for k in range(0, BASIS, 3):
+                part = jnp.dot(
+                    tfwd[k : k + 3].reshape(3 * WIDE, EXT),
+                    first[SIDE * side : SIDE * side + EXT],
+                    preferred_element_type=F32,
+                )
+                zw[side, k : k + 3] = part.astype(BF16).reshape(3, WIDE, CH)
+
+    def mix_wide(side):
+        total = jnp.zeros((WIDE, CH), F32)
+        for k in range(BASIS):
+            total += jnp.dot(zw[side, k], wf[0, k], preferred_element_type=F32)
+        at = SIDE * (side + 1) + 16
+        base = first[at : at + WIDE, :].astype(F32)
+        at = SIDE * side + 16
+        xs[0, at : at + WIDE, :] = (base + gelu_and_slope(total)[0]).astype(BF16)
+        if side == 1:
+            yb[...] = total[16 : 16 + CELLS]
+
     def spread_x(layer):
-        xt[layer] = xs[layer].astype(F32).T.astype(BF16)
+        field = xs[0] if layer else first[SIDE : SIDE + EXT]
+        xt[layer] = field.astype(F32).T.astype(BF16)
         xg[layer, x] = xt[layer, pl.ds(pl.multiple_of(x * 64, 64), 64)]
 
         def block(d):
@@ -322,7 +369,7 @@
         for k in range(0, BASIS, 3):
             part = lax.dot_general(
                 xg[layer].reshape(NX * 64, EXT),
-                tmap[0, k : k + 3].reshape(3 * CELLS, EXT),
+                tfwd[k : k + 3, 16 : 16 + CELLS].reshape(3 * CELLS, EXT),
                 (((1,), (1,)), ((), ())),
                 preferred_element_type=F32,
             ).astype(BF16)
@@ -358,10 +405,10 @@
         return total
 
     def own_block(n):
-        return xs[n, OWN : OWN + CELLS, :].astype(F32)
+        return xs[n - 1, OWN : OWN + CELLS, :].astype(F32)
 
     def spread_s(layer, n, values):
-        xs[n, OWN : OWN + CELLS, :] = values
+        xs[n - 1, OWN : OWN + CELLS, :] = values
         if layer:
             around = halo(n)
         for h in range(2):
@@ -376,9 +423,9 @@
                 if d == 0 and dc == 0:
                     continue
                 h = core if dc == 0 else other
-                src = xs.at[n, OWN : OWN + CELLS, pl.ds(pl.multiple_of(h * 128, 128), 128)]
+                src = xs.at[n - 1, OWN : OWN + CELLS, pl.ds(pl.multiple_of(h * 128, 128), 128)]
                 copies.append((src, sg.at[layer, x, core], (lat if dc == 0 else sib, at_x(d))))
-        spread = send(copies, xs.at[n, 0 : 7 * CELLS // 2])
+        spread = send(copies, xs.at[n - 1, 0 : 7 * CELLS // 2])
         if not layer:
             around = halo(n)
         return around, spread
@@ -439,30 +486,26 @@
     build(1)
     next(gather2)
     arrive(in_halo)
-    conv(0, 0)
+    conv_wide()
+    z1 = spread_x(0)
+    next(z1)
     next(gather1)
     next(gather1, None)
     settle(0)
-    y1 = mix(0)
-    yb[...] = y1
-    hidden = (own_block(0) + gelu_and_slope(y1)[0]).astype(BF16)
-    xs[1, OWN : OWN + CELLS, :] = hidden
-    mid_halo = halo(1)
-    z1 = spread_x(0)
-    next(z1)
+    for side in range(3):
+        mix_wide(side)
     next(gather2)
+    z2 = spread_x(1)
+    next(z2)
+    conv(0, 1)
     next(gather2, None)
     settle(1)
-    next(z1)
-    arrive(mid_halo)
-    conv(0, 1)
-    z2 = spread_x(1)
-    next(z2)
     y2 = mix(1)
     grown, slope = gelu_and_slope(y2)
     loads[6].wait()
     around2, all_s2 = spread_s(1, 2, (cot[...].astype(F32) * slope).astype(BF16))
     out_ref[...] = (own_block(1) + grown).astype(BF16)
+    next(z1)
     next(z2)
     arrive(around2)
     conv(1, 2)
@@ -470,9 +513,9 @@
     s1 = (grad_hidden * gelu_and_slope(yb[...])[1]).astype(BF16)
     around1, all_s1 = spread_s(0, 3, s1)
     arrive(all_s2)
-    next(z1, None)
     next(z2, None)
     p2 = weight_partial(1)
+    next(z1, None)
     arrive(all_s1)
     p1 = weight_partial(0)
     arrive(around1)
@@ -515,12 +558,15 @@
             pltpu.VMEM((CELLS, CH), BF16),
             pltpu.VMEM((BASIS, 128, GRID), F32),
             pltpu.VMEM((ROWS + 4, BASIS, 8, 128), F32),
-            pltpu.VMEM((8, BASIS, 16, 256), F32),
-            pltpu.VMEM((2, BASIS, CELLS, EXT), BF16),
-            pltpu.VMEM((4, EXT, CH), BF16),
+            pltpu.VMEM((10, BASIS, 16, 256), F32),
+            pltpu.VMEM((BASIS, WIDE, EXT), BF16),
+            pltpu.VMEM((BASIS, CELLS, EXT), BF16),
+            pltpu.VMEM((FIRST, CH), BF16),
+            pltpu.VMEM((3, EXT, CH), BF16),
             pltpu.VMEM((2, 2, NX, NY, BASIS, 8, 128), BF16),
             pltpu.VMEM((2, BASIS, CH, CH), BF16),
             pltpu.VMEM((BASIS, CELLS, CH), BF16),
+            pltpu.VMEM((3, BASIS, WIDE, CH), BF16),
             pltpu.VMEM((2, CH, EXT), BF16),
             pltpu.VMEM((2, NX, 64, EXT), BF16),
             pltpu.VMEM((2, NX, 2, BASIS, 64, CELLS), BF16),

time: 69.4 us -> 73.9 us (1.065)
  Pallas kernels: 68.6 us -> 73.1 us
    pallas_call x1, Pallas kernels: 66.9 us -> 71.4 us  [local(): pl.pallas_call(kernel, out_shape=shapes, in_specs=[hbm] * 7, out_specs=(v...]
where the time goes in v4:
time: 73.9 us; the launch traced here: 73.7 us
  Pallas kernels  73.1 us (99%)
    pallas_call x1, Pallas kernels, local(): pl.pallas_call(kernel, out_shape=shapes, in_specs=[hbm] * 7, out_specs=(v...  71.4 us
    pallas_call x1, Pallas kernels, local(): pl.pallas_call(deliver, out_shape=shapes, in_specs=[vmem] * 4, out_specs=...  1.7 us

profile of v4, /device:TPU:1, one launch (start us, length us, event | category | flops | bytes accessed | tf_op | source)
XLA Modules:
  0.0 73.7 jit_solution(15666524762477083119)
XLA Ops:
  0.6 71.4 %shard_map.102 = (bf16[128,256]{1,0:T(8,128)(2,1)}, bf16[128,256]{1,0:T(8,128)(2,1)}, f32[9,8,256]{2,1,0:T(8,128)}, f32[9,8,256]{2,1,0:T(8,128)}) custom-call(bf16[128,256]{1,0:T(8,128)(2,1)} %bitcast.6, bf16[9,5,17,256]{3,2,1,0:T(8,128)(2,1)} %bitcast.5, s32[256]{0:T(256)} %depth_ref.1, s32[256]{0:T(256)} %extent_ref.1, bf16[9,8,256]{2,1,0:T(8,128)(2,1)} %w1_ref.1, ...), custom_call_target="tpu_custom_call" | custom-call | flops 1000000000 | bytes 10000000 | tf_op jit(solution)/shard_map/pallas_call | solution.py:549
  72.0 1.7 %shard_map.103 = (bf16[128,256]{1,0:T(8,128)(2,1)}, bf16[128,256]{1,0:T(8,128)(2,1)}, f32[9,8,256]{2,1,0:T(8,128)}, f32[9,8,256]{2,1,0:T(8,128)}) custom-call(bf16[128,256]{1,0:T(8,128)(2,1)} %get-tuple-element.12.refs_0_, bf16[128,256]{1,0:T(8,128)(2,1)} %get-tuple-element.13.refs_1_, f32[9,8,256]{2,1,0:T(8,128)} %get-tuple-element.14.refs_2_, ...), custom_call_target="tpu_custom_call" | custom-call | tf_op jit(solution)/shard_map/pallas_call | solution.py:597

commit v5 on v3

--- a/solution.py
+++ b/solution.py
@@ -453,22 +453,22 @@
     next(gather2)
     next(gather2, None)
     settle(1)
-    next(z1)
     arrive(mid_halo)
     conv(0, 1)
-    z2 = spread_x(1)
-    next(z2)
     y2 = mix(1)
     grown, slope = gelu_and_slope(y2)
     loads[6].wait()
     around2, all_s2 = spread_s(1, 2, (cot[...].astype(F32) * slope).astype(BF16))
+    z2 = spread_x(1)
+    next(z2)
     out_ref[...] = (own_block(1) + grown).astype(BF16)
-    next(z2)
+    next(z1)
     arrive(around2)
     conv(1, 2)
     grad_hidden = (cot[...].astype(F32) + mix_back(1)).astype(BF16).astype(F32)
     s1 = (grad_hidden * gelu_and_slope(yb[...])[1]).astype(BF16)
     around1, all_s1 = spread_s(0, 3, s1)
+    next(z2)
     arrive(all_s2)
     next(z1, None)
     next(z2, None)

time: 69.4 us -> 70 us (level)
  no operation moved by 1% of the time
where the time goes in v5:
time: 70 us; the launch traced here: 69.8 us
  Pallas kernels  69.2 us (99%)
    pallas_call x1, Pallas kernels, local(): pl.pallas_call(kernel, out_shape=shapes, in_specs=[hbm] * 7, out_specs=(v...  67.5 us
    pallas_call x1, Pallas kernels, local(): pl.pallas_call(deliver, out_shape=shapes, in_specs=[vmem] * 4, out_specs=...  1.7 us

profile of v5, /device:TPU:1, one launch (start us, length us, event | category | flops | bytes accessed | tf_op | source)
XLA Modules:
  0.0 69.8 jit_solution(10615878604132408933)
XLA Ops:
  0.6 67.5 %shard_map.102 = (bf16[128,256]{1,0:T(8,128)(2,1)}, bf16[128,256]{1,0:T(8,128)(2,1)}, f32[9,8,256]{2,1,0:T(8,128)}, f32[9,8,256]{2,1,0:T(8,128)}) custom-call(bf16[128,256]{1,0:T(8,128)(2,1)} %bitcast.6, bf16[9,5,17,256]{3,2,1,0:T(8,128)(2,1)} %bitcast.5, s32[256]{0:T(256)} %depth_ref.1, s32[256]{0:T(256)} %extent_ref.1, bf16[9,8,256]{2,1,0:T(8,128)(2,1)} %w1_ref.1, ...), custom_call_target="tpu_custom_call" | custom-call | flops 1000000000 | bytes 10000000 | tf_op jit(solution)/shard_map/pallas_call | solution.py:506
  68.1 1.7 %shard_map.103 = (bf16[128,256]{1,0:T(8,128)(2,1)}, bf16[128,256]{1,0:T(8,128)(2,1)}, f32[9,8,256]{2,1,0:T(8,128)}, f32[9,8,256]{2,1,0:T(8,128)}) custom-call(bf16[128,256]{1,0:T(8,128)(2,1)} %get-tuple-element.12.refs_0_, bf16[128,256]{1,0:T(8,128)(2,1)} %get-tuple-element.13.refs_1_, f32[9,8,256]{2,1,0:T(8,128)} %get-tuple-element.14.refs_2_, ...), custom_call_target="tpu_custom_call" | custom-call | tf_op jit(solution)/shard_map/pallas_call | solution.py:551

commit v6 on v3

--- a/solution.py
+++ b/solution.py
@@ -16,9 +16,9 @@
 OWN = SIDE + 2 * COLS
 F32 = jnp.float32
 BF16 = jnp.bfloat16
-SLOTS = 60
+SLOTS = 44
 SPLIT = 2
-PARTS, DEEP = 3, 3
+PARTS = (3, 1)
 
 
 def gelu_and_slope(y):
@@ -385,52 +385,56 @@
 
     def weight_partial(layer):
         groups = []
-        for c in range(PARTS):
-            total = jnp.zeros((DEEP * 64, 128), F32)
-            ks = slice(DEEP * c, DEEP * c + DEEP)
+        deep = BASIS // PARTS[layer]
+        for k in range(0, BASIS, deep):
+            total = jnp.zeros((deep * 64, 128), F32)
+            ks = slice(k, k + deep)
             for a in range(NX):
                 left = jnp.concatenate(
-                    [zg[layer, a, h, ks].reshape(DEEP * 64, 128) for h in range(2)], axis=1
+                    [zg[layer, a, h, ks].reshape(deep * 64, 128) for h in range(2)], axis=1
                 )
                 total += jnp.dot(left, sg[layer, a].reshape(256, 128), preferred_element_type=F32)
-            blocks = total.reshape(DEEP, NY, 8, 128)
+            blocks = total.reshape(deep, NY, 8, 128)
             for b in range(NY):
-                pb[layer, c, b] = blocks[:, b].astype(BF16)
-            ry[layer, c, y] = pb[layer, c, y]
+                pb[layer, b, ks] = blocks[:, b].astype(BF16)
+            ry[layer, y, ks] = pb[layer, y, ks]
             groups.append(
                 send(
                     [
-                        (pb.at[layer, c, lax.rem(y + d, NY)], ry.at[layer, c, y], (lat, at_y(d)))
+                        (pb.at[layer, lax.rem(y + d, NY), ks], ry.at[layer, y, ks], (lat, at_y(d)))
                         for d in (4, 3, 5, 2, 6, 1, 7)
                     ],
-                    ry.at[layer, c, 0 : NY - 1],
+                    ry.at[layer, 0 : NY - 1, ks],
                 )
             )
         return groups
 
     def weight_rows(layer, got):
         groups = []
-        for c in range(PARTS):
-            arrive(got[c])
-            qy[layer, c] = jnp.sum(ry[layer, c].astype(F32), axis=0).astype(BF16)
-            rz[layer, c, z] = qy[layer, c]
+        deep = BASIS // PARTS[layer]
+        for c, group in enumerate(got):
+            arrive(group)
+            ks = slice(deep * c, deep * c + deep)
+            qy[layer, ks] = jnp.sum(ry[layer, :, ks].astype(F32), axis=0).astype(BF16)
+            rz[layer, z, ks] = qy[layer, ks]
             groups.append(
                 send(
                     [
-                        (qy.at[layer, c], rz.at[layer, c, z], (at_z(d), lon))
+                        (qy.at[layer, ks], rz.at[layer, z, ks], (at_z(d), lon))
                         for d in (4, 3, 5, 2, 6, 1, 7)
                     ],
-                    rz.at[layer, c, 0 : NZ - 1],
+                    rz.at[layer, 0 : NZ - 1, ks],
                 )
             )
         return groups
 
     def weight_bands(layer, got):
         groups = []
-        for c in range(PARTS):
-            arrive(got[c])
-            ks = slice(DEEP * c, DEEP * c + DEEP)
-            fin[layer, core, ks] = jnp.sum(rz[layer, c].astype(F32), axis=0)
+        deep = BASIS // PARTS[layer]
+        for c, group in enumerate(got):
+            arrive(group)
+            ks = slice(deep * c, deep * c + deep)
+            fin[layer, core, ks] = jnp.sum(rz[layer, :, ks].astype(F32), axis=0)
             mine = fin.at[layer, core, ks]
             groups.append(send([(mine, mine, (sib, lon))], mine))
         return groups
@@ -453,7 +457,6 @@
     next(gather2)
     next(gather2, None)
     settle(1)
-    next(z1)
     arrive(mid_halo)
     conv(0, 1)
     z2 = spread_x(1)
@@ -463,6 +466,7 @@
     loads[6].wait()
     around2, all_s2 = spread_s(1, 2, (cot[...].astype(F32) * slope).astype(BF16))
     out_ref[...] = (own_block(1) + grown).astype(BF16)
+    next(z1)
     next(z2)
     arrive(around2)
     conv(1, 2)
@@ -525,10 +529,10 @@
             pltpu.VMEM((2, NX, 64, EXT), BF16),
             pltpu.VMEM((2, NX, 2, BASIS, 64, CELLS), BF16),
             pltpu.VMEM((2, NX, 2, CELLS, 128), BF16),
-            pltpu.VMEM((2, PARTS, NY, DEEP, 8, 128), BF16),
-            pltpu.VMEM((2, PARTS, NY, DEEP, 8, 128), BF16),
-            pltpu.VMEM((2, PARTS, DEEP, 8, 128), BF16),
-            pltpu.VMEM((2, PARTS, NZ, DEEP, 8, 128), BF16),
+            pltpu.VMEM((2, NY, BASIS, 8, 128), BF16),
+            pltpu.VMEM((2, NY, BASIS, 8, 128), BF16),
+            pltpu.VMEM((2, BASIS, 8, 128), BF16),
+            pltpu.VMEM((2, NZ, BASIS, 8, 128), BF16),
             pltpu.VMEM((2, 2, BASIS, 8, 128), F32),
             pltpu.VMEM((CELLS, CH), F32),
             pltpu.SemaphoreType.DMA((SLOTS,)),

time: 69.4 us -> 68.4 us (0.986)
  Pallas kernels: 68.6 us -> 67.6 us
    pallas_call x1, Pallas kernels: 66.9 us -> 65.9 us  [local(): pl.pallas_call(kernel, out_shape=shapes, in_specs=[hbm] * 7, out_specs=(v...]
where the time goes in v6:
time: 68.4 us; the launch traced here: 68.2 us
  Pallas kernels  67.6 us (99%)
    pallas_call x1, Pallas kernels, local(): pl.pallas_call(kernel, out_shape=shapes, in_specs=[hbm] * 7, out_specs=(v...  65.9 us
    pallas_call x1, Pallas kernels, local(): pl.pallas_call(deliver, out_shape=shapes, in_specs=[vmem] * 4, out_specs=...  1.7 us

profile of v6, /device:TPU:1, one launch (start us, length us, event | category | flops | bytes accessed | tf_op | source)
XLA Modules:
  0.0 68.2 jit_solution(3155733167000878141)
XLA Ops:
  0.6 65.9 %shard_map.102 = (bf16[128,256]{1,0:T(8,128)(2,1)}, bf16[128,256]{1,0:T(8,128)(2,1)}, f32[9,8,256]{2,1,0:T(8,128)}, f32[9,8,256]{2,1,0:T(8,128)}) custom-call(bf16[128,256]{1,0:T(8,128)(2,1)} %bitcast.6, bf16[9,5,17,256]{3,2,1,0:T(8,128)(2,1)} %bitcast.5, s32[256]{0:T(256)} %depth_ref.1, s32[256]{0:T(256)} %extent_ref.1, bf16[9,8,256]{2,1,0:T(8,128)(2,1)} %w1_ref.1, ...), custom_call_target="tpu_custom_call" | custom-call | flops 1000000000 | bytes 10000000 | tf_op jit(solution)/shard_map/pallas_call | solution.py:510
  66.5 1.7 %shard_map.103 = (bf16[128,256]{1,0:T(8,128)(2,1)}, bf16[128,256]{1,0:T(8,128)(2,1)}, f32[9,8,256]{2,1,0:T(8,128)}, f32[9,8,256]{2,1,0:T(8,128)}) custom-call(bf16[128,256]{1,0:T(8,128)(2,1)} %get-tuple-element.12.refs_0_, bf16[128,256]{1,0:T(8,128)(2,1)} %get-tuple-element.13.refs_1_, f32[9,8,256]{2,1,0:T(8,128)} %get-tuple-element.14.refs_2_, ...), custom_call_target="tpu_custom_call" | custom-call | tf_op jit(solution)/shard_map/pallas_call | solution.py:555
